TPU v7x, 128 devices: a whole 4x4x4 slice. The times are simulated.
128 devices in a mesh: row: 8 (over y, core), col: 16 (over z, x).
Axes of the slice: x: 4, y: 4, z: 4, core: 2. Of those that a mesh axis runs over, the one named last changes fastest.
Arguments:
- user_factors: float32 [16384, 128], P('row'), may hold values from -6 to 6
- item_factors: float32 [131072, 128], P(('row', 'col')), may hold values from -0.015625 to 0.015625
- fetch_list: int32 [8, 16, 128, 1], P('row', 'col'), may hold values from 0 to 7
- tile_user: int32 [8, 16, 32], P('row', 'col'), may hold values from 0 to 15
- tile_slot: int32 [8, 16, 32], P('row', 'col'), may hold values from 0 to 127
- entry_row: int32 [8, 16, 32, 512], P('row', 'col'), may hold values from 0 to 127
- entry_col: int32 [8, 16, 32, 512], P('row', 'col'), may hold values from 0 to 127
- entry_count: int32 [8, 16, 32, 512], P('row', 'col'), may hold values from 1 to 8
- tile_count: int32 [8, 16], P('row', 'col'), may hold values from 4 to 32, as said below
Outputs:
- solved: float32 [16384, 128], P('row')
Inputs may be any that keep to these rules, and one draw needn't show every extreme that they name: `tile_count`: at least 4 tiles live on every device; some device has all 32 live in every draw.
All inputs are finite; a program needn't handle non-finite values.
Results may differ from a plain program's by a relative error of at most 0.0003.
Values sent between devices are 32-bit elements; how exact they have to be, the bound alone decides.
A program may use at most 128 MiB of HBM per device.

v0:
```python
import jax
import jax.numpy as jnp
from jax import lax
from jax.sharding import PartitionSpec as P

K = 128
BLOCK = 128
ITERS = 3


HIGHEST = lax.Precision.HIGHEST
CONFIDENCE_SCALE = 40.0
RIDGE = 0.5
EPSILON = 1e-06


def conjugate(iterate, residual, apply_full):
    direction = residual
    norm_now = jnp.sum(residual * residual, axis=1, keepdims=True)
    for iteration in range(ITERS):
        image = apply_full(direction)
        alpha = norm_now / (jnp.sum(direction * image, axis=1, keepdims=True) + EPSILON)
        iterate = iterate + alpha * direction
        residual = residual - alpha * image
        norm_next = jnp.sum(residual * residual, axis=1, keepdims=True)
        direction = residual + norm_next / (norm_now + EPSILON) * direction
        norm_now = norm_next
    return iterate


def shards(
    user_factors,
    item_factors,
    fetch_list,
    tile_user,
    tile_slot,
    entry_row,
    entry_col,
    entry_count,
    tile_count,
):
    user_rows = user_factors.shape[0]
    user_blocks = user_rows // BLOCK
    local_blocks = item_factors.reshape(-1, BLOCK, K)
    wanted = fetch_list[0, 0]
    peers = wanted.shape[0]
    width = wanted.shape[1]
    asked = lax.all_to_all(wanted, ("row", "col"), split_axis=0, concat_axis=0, tiled=True)
    served = jnp.take(local_blocks, asked.reshape(-1), axis=0).reshape(peers, width, BLOCK, K)
    fetched = lax.all_to_all(
        served, ("row", "col"), split_axis=0, concat_axis=0, tiled=True
    ).reshape(-1, BLOCK, K)
    gram = lax.psum(
        jnp.dot(
            item_factors.T, item_factors, precision=HIGHEST, preferred_element_type=jnp.float32
        ),
        ("row", "col"),
    )
    users = tile_user[0, 0]
    slot_ids = tile_slot[0, 0]
    tiles = users.shape[0]
    tile_index = jnp.arange(tiles, dtype=jnp.int32)
    alive = (tile_index < tile_count[0, 0]).astype(jnp.float32)
    excess = CONFIDENCE_SCALE * entry_count[0, 0].astype(jnp.float32)
    weight_fit = excess * alive[:, None]
    weight_rhs = (1.0 + excess) * alive[:, None]
    rows_in = entry_row[0, 0]
    cols_in = entry_col[0, 0]
    block_ids = jnp.arange(BLOCK, dtype=jnp.int32)
    row_onehot = (rows_in[:, :, None] == block_ids[None, None, :]).astype(jnp.float32)
    col_onehot = (cols_in[:, :, None] == block_ids[None, None, :]).astype(jnp.float32)
    dense_fit = jnp.einsum(
        "tnu,tni->tui", row_onehot * weight_fit[:, :, None], col_onehot, precision=HIGHEST
    )
    dense_rhs = jnp.einsum(
        "tnu,tni->tui", row_onehot * weight_rhs[:, :, None], col_onehot, precision=HIGHEST
    )
    item_tiles = jnp.take(fetched, slot_ids, axis=0)
    owner_onehot = (users[None, :] == jnp.arange(user_blocks, dtype=jnp.int32)[:, None]).astype(
        jnp.float32
    )

    def tile_terms(vector):
        picked_users = jnp.take(vector.reshape(user_blocks, BLOCK, K), users, axis=0)
        scores = jnp.einsum("tuk,tik->tui", picked_users, item_tiles, precision=HIGHEST)
        pulled = jnp.einsum("tui,tik->tuk", dense_fit * scores, item_tiles, precision=HIGHEST)
        return jnp.einsum("bt,tuk->buk", owner_onehot, pulled, precision=HIGHEST).reshape(
            user_rows, K
        )

    rhs_pulled = jnp.einsum("tui,tik->tuk", dense_rhs, item_tiles, precision=HIGHEST)
    rhs_local = jnp.einsum("bt,tuk->buk", owner_onehot, rhs_pulled, precision=HIGHEST).reshape(
        user_rows, K
    )

    def extra(vector):
        return (
            jnp.dot(vector, gram, precision=HIGHEST, preferred_element_type=jnp.float32)
            + RIDGE * vector
        )

    start_terms = rhs_local - tile_terms(user_factors)

    def apply_whole(vector):
        return lax.psum(tile_terms(vector), "col") + extra(vector)

    residual = lax.psum(start_terms, "col") - extra(user_factors)
    solved = conjugate(user_factors, residual, apply_whole)
    return solved


def solution(mesh):
    return jax.shard_map(
        shards,
        mesh=mesh,
        in_specs=(
            P("row", None),
            P(("row", "col"), None),
            P("row", "col", None, None),
            P("row", "col", None),
            P("row", "col", None),
            P("row", "col", None, None),
            P("row", "col", None, None),
            P("row", "col", None, None),
            P("row", "col"),
        ),
        out_specs=P("row", None),
        check_vma=False,
    )
```

profile of v0, /device:TPU:0, one launch (start us, length us, event | category | flops | bytes accessed | tf_op | source)
XLA Modules:
  0.0 695.5 jit_solution(1226374862709490610)
XLA Ops:
  6.5 0.8 copy.50
  7.4 20.4 %all_to_all.20 = s32[128,1,1]{2,1,0:T(1,128)S(1)} all-to-all(s32[128,1,1]{2,1,0:T(1,128)S(1)} %copy.50), channel_id=1, replica_groups=mesh['row'=8,'col'=16] {'row','col'}, dimensions={0} | all-to-all | bytes 1024 | tf_op jit(solution)/shard_map/all_to_all | solution.py:48
  27.8 2.3 reduce
  30.2 4.3 gather_fusion
  34.5 7.2 %bitcast_select_fusion = f32[128,1,128,128]{3,2,1,0:T(8,128)} fusion(f32[128,128,128]{2,1,0:T(8,128)} %gather_fusion, pred[128]{0:T(512)(128)(4,1)S(1)} %compare_and_fusion.1), kind=kLoop, calls=%fused_computation.6 | loop fusion | flops 2097152 | bytes 16777344 | tf_op jit(solution)/shard_map/jit(_take)/select_n | solution.py:49
  41.7 6.1 all-to-all-start.1
  47.8 0.0 all-reduce.8.cloned.1.call-start
  47.8 1.6 fusion.103
  49.5 0.0 all-reduce.8.cloned.1.call-update
  49.5 0.0 all-reduce.6.cloned.1.call-start
  50.3 2.0 gather_fusion.2
  52.3 0.1 fusion.75
  52.4 8.1 %fusion = f32[32,128,128]{2,1,0:T(8,128)} fusion(f32[32,512]{1,0:T(8,128)S(1)} %get-tuple-element.11, s32[32,512]{1,0:T(8,128)S(1)} %bitcast.99, s32[32,512]{1,0:T(8,128)S(1)} %bitcast.101), kind=kOutput, calls=%fused_computation.7 | convolution fusion | flops 3227516928 | bytes 2293760 | tf_op jit(solution)/shard_map/tnu,tni->tui/dot_general | solution.py:72
  60.5 8.2 %fusion.2 = f32[32,128,128]{2,1,0:T(8,128)} fusion(s32[32,512]{1,0:T(8,128)S(1)} %bitcast.100, f32[32,512]{1,0:T(8,128)S(1)} %get-tuple-element.10, s32[32,512]{1,0:T(8,128)S(1)} %bitcast.102), kind=kOutput, calls=%fused_computation.10 | convolution fusion | flops 3227516928 | bytes 2293760 | tf_op jit(solution)/shard_map/tnu,tni->tui/dot_general | solution.py:75
  68.8 79.1 %all-to-all-done.1 = f32[128,1,128,128]{3,2,1,0:T(8,128)} async-done(((f32[128,1,128,128]{3,2,1,0:T(8,128)}), f32[128,1,128,128]{3,2,1,0:T(8,128)}, u32[]{:S(2)}, u32[]{:S(2)}) %all-to-all-start.1) | async-done | bytes 8388640 | tf_op jit(solution)/shard_map/all_to_all | solution.py:50
  147.9 4.1 gather_fusion.1
  152.0 3.9 fusion.50
  155.9 4.6 fusion.28
  160.5 2.3 fusion.36
  162.8 2.0 fusion.18
  164.8 2.2 fusion.38
  167.1 1.3 copy.53
  168.4 2.6 copy.54
  171.0 0.0 all-reduce.10.cloned.1.call-start
  171.0 1.3 copy.60
  172.3 81.8 %all-reduce.8.cloned.1.call-done = f32[128,128]{1,0:T(8,128)} async-done(((f32[128,128]{1,0:T(8,128)}), f32[128,128]{1,0:T(8,128)}) %all-reduce.8.cloned.1.call-update) | async-done | bytes 65552 | tf_op jit(solution)/shard_map/psum | solution.py:53
  254.1 90.1 %all-reduce.6.cloned.1.call-done = f32[2048,128]{0,1:T(8,128)} async-done(((f32[2048,128]{0,1:T(8,128)}), f32[2048,128]{0,1:T(8,128)}) %all-reduce.6.cloned.1.call-update) | async-done | bytes 1048592 | tf_op jit(solution)/shard_map/psum | solution.py:107
  344.2 3.0 fusion.13
  347.2 1.3 copy.77
  348.5 3.2 gather_fusion.3
  351.7 6.3 fusion.26
  358.0 3.6 fusion.34
  361.7 3.1 copy.69
  364.8 2.4 fusion.81
  367.2 1.4 copy.97
  368.5 0.4 all-reduce.12.cloned.1.call-start
  369.0 86.0 %all-reduce.10.cloned.1.call-done = f32[2048,128]{0,1:T(8,128)} async-done(((f32[2048,128]{0,1:T(8,128)}), f32[2048,128]{0,1:T(8,128)}) %all-reduce.10.cloned.1.call-update) | async-done | bytes 1048592 | tf_op jit(solution)/shard_map/psum | solution.py:105
  455.0 2.5 multiply_reduce_fusion.3
  457.5 0.2 multiply_reduce_fusion.2
  457.7 1.0 copy-done.8
  458.7 1.1 multiply_add_fusion.2
  459.9 2.6 copy.79
  462.4 3.2 gather_fusion.4
  465.6 6.3 fusion.24
  472.0 3.6 fusion.32
  475.6 3.1 copy.72
  478.7 2.4 fusion.79
  481.1 1.4 copy.96
  482.4 0.2 all-reduce.14.cloned.1.call-start
  482.7 86.2 %all-reduce.12.cloned.1.call-done = f32[2048,128]{0,1:T(8,128)} async-done(((f32[2048,128]{0,1:T(8,128)}), f32[2048,128]{0,1:T(8,128)}) %all-reduce.12.cloned.1.call-update) | async-done | bytes 1048592 | tf_op jit(solution)/shard_map/psum | solution.py:105
  568.8 3.2 multiply_reduce_fusion.1
  572.1 0.2 multiply_reduce_fusion
  572.3 1.2 multiply_add_fusion.1
  573.6 2.5 copy.81
  576.1 3.2 gather_fusion.5
  579.3 6.3 fusion.22
  585.6 3.6 fusion.30
  589.2 2.4 copy.75
  591.6 0.8 fusion.77
  592.5 1.3 copy.95
  593.8 86.4 %all-reduce.14.cloned.1.call-done = f32[2048,128]{0,1:T(8,128)} async-done(((f32[2048,128]{0,1:T(8,128)}), f32[2048,128]{0,1:T(8,128)}) %all-reduce.14.cloned.1.call-update) | async-done | bytes 1048592 | tf_op jit(solution)/shard_map/psum | solution.py:105
  680.2 3.0 fusion.41
  683.3 3.0 multiply_add_fusion
  686.3 2.5 copy.68
  (54 shorter events, 0.2 us)
Async XLA Ops:
  6.5 23.6 %copy-start = (f32[1024,128]{1,0:T(8,128)S(1)}, f32[1024,128]{1,0:T(8,128)}, u32[]{:S(2)}) copy-start(f32[1024,128]{1,0:T(8,128)} %param.12) | copy-start | bytes 1572868
  41.7 8.5 %copy-start.14 = (s32[1,1,32]{2,1,0:T(1,128)S(1)}, s32[1,1,32]{2,1,0:T(1,128)}, u32[]{:S(2)}) copy-start(s32[1,1,32]{2,1,0:T(1,128)} %param.14) | copy-start | bytes 388
  41.7 106.2 %all-to-all-start.1 = ((f32[128,1,128,128]{3,2,1,0:T(8,128)}), f32[128,1,128,128]{3,2,1,0:T(8,128)}, u32[]{:S(2)}, u32[]{:S(2)}) async-start(f32[128,1,128,128]{3,2,1,0:T(8,128)} %bitcast_select_fusion), calls=%async_computation.1 | async-start | bytes 16777216 | tf_op jit(solution)/shard_map/all_to_all | solution.py:50
  47.8 2.5 copy-start.10
  47.8 206.3 %all-reduce.8.cloned.1.call-start = ((), (), s32[]{:S(2)}) async-start(), calls=%async_computation.3 | async-start | bytes 131072 | tf_op jit(solution)/shard_map/psum | solution.py:53
  49.5 294.7 %all-reduce.6.cloned.1.call-start = ((), (), s32[]{:S(2)}) async-start(), calls=%async_computation.2 | async-start | bytes 2097152 | tf_op jit(solution)/shard_map/psum | solution.py:107
  50.2 2.0 copy-start.15
  50.3 2.1 copy-start.13
  50.3 2.2 copy-start.16
  50.3 2.2 copy-start.17
  151.9 4.0 copy-start.11
  155.9 4.6 copy-start.2
  171.0 284.0 %all-reduce.10.cloned.1.call-start = ((), (), s32[]{:S(2)}) async-start(), calls=%async_computation.4 | async-start | bytes 2097152 | tf_op jit(solution)/shard_map/psum | solution.py:105
  351.7 6.3 copy-start.3
  367.2 87.8 %copy-start.12 = (f32[128,128]{1,0:T(8,128)S(1)}, f32[128,128]{1,0:T(8,128)}, u32[]{:S(2)}) copy-start(f32[128,128]{1,0:T(8,128)} %all-reduce.8.cloned.1.call-done) | copy-start | bytes 196612
  368.5 200.3 %all-reduce.12.cloned.1.call-start = ((), (), s32[]{:S(2)}) async-start(), calls=%async_computation.5 | async-start | bytes 2097152 | tf_op jit(solution)/shard_map/psum | solution.py:105
  457.7 1.0 copy-start.8
  465.6 6.3 copy-start.4
  482.4 197.8 %all-reduce.14.cloned.1.call-start = ((), (), s32[]{:S(2)}) async-start(), calls=%async_computation.6 | async-start | bytes 2097152 | tf_op jit(solution)/shard_map/psum | solution.py:105
  568.8 3.3 copy-start.9
  568.8 3.5 copy-start.6
  579.3 6.3 copy-start.5
  593.8 89.5 %copy-start.7 = (f32[2048,128]{0,1:T(8,128)S(1)}, f32[2048,128]{0,1:T(8,128)}, u32[]{:S(2)}) copy-start(f32[2048,128]{0,1:T(8,128)} %multiply_add_fusion.2) | copy-start | bytes 3145732
  683.3 5.5 copy-start.1
Sparse Core Ops, SparseCore 0:
  53.4 200.6 all-reduce.7
  257.7 86.4 all-reduce.5
  368.7 86.2 all-reduce.9
  482.6 86.2 all-reduce.11
  593.9 86.2 all-reduce.13
where the time goes:
time: 702 us; the launch traced here: 696 us
  waiting for transfers between devices  510 us (73%)
  matrix products  80.1 us (11%)
  local copies, waits for them, and re-layouts  48.6 us (7%)
  blocking collectives  20.4 us (3%)
  other arithmetic  15.5 us (2%)
  between operations  14.4 us (2%)
    psum x3, waiting for transfers between devices, apply_whole(): return lax.psum(tile_terms(vector), 'col') + extra(vector)  259 us
    psum x1, waiting for transfers between devices, shards(): residual = lax.psum(start_terms, 'col') - extra(user_factors)  90.1 us
    psum x1, waiting for transfers between devices, shards(): lax.psum(jnp.dot(item_factors.T, item_factors, precision=HIGHEST, preferr...  81.8 us
    all_to_all x1, waiting for transfers between devices, shards(): lax.all_to_all(served, ('row', 'col'), split_axis=0, concat_axis=0, tiled...  79.1 us
    dot_general x4, matrix products, tile_terms(): jnp.einsum('tuk,tik->tui', picked_users, item_tiles, precision=HIGHEST)  23.5 us
    all_to_all x1, blocking collectives, shards(): lax.all_to_all(wanted, ('row', 'col'), split_axis=0, concat_axis=0, tiled...  20.4 us
  transfers between devices with their start and end apart: 6, of which 6 were waited for; matrix products, arithmetic and copies ran while one was open for 6% of the time, Pallas kernels for 0%

commit v1 on v0

v1 whole, which is shorter than its diff:
```python
import functools

import jax
import jax.numpy as jnp
from jax import lax
from jax.experimental import pallas as pl
from jax.experimental.pallas import tpu as pltpu
from jax.sharding import PartitionSpec as P

K = 128
BLOCK = 128
UB = 16
IB = 8
TILES = 32
NNZ = 512
NZ = NX = 4
NY = 4
ROWS = 8
COLS = 16
ALL_TILES = COLS * TILES
LIST = 1024
GROUP = 4
HELD = 32
STAGE = 3 * TILES + 8
HALF = 56
SCALE = 40.0
RIDGE = 0.5
EPSILON = 1e-06
MESH = pl.DeviceIdType.MESH
F32 = jnp.float32
BF16 = jnp.bfloat16
NT = (((1,), (1,)), ((), ()))
TN = (((0,), (0,)), ((), ()))
NN = (((1,), (0,)), ((), ()))
ANY = pl.BlockSpec(memory_space=pl.ANY)
VMEM = pl.BlockSpec(memory_space=pltpu.VMEM)
SMEM = pl.BlockSpec(memory_space=pltpu.SMEM)
BIG = 48 * 2**20


def dot(a, b, dims):
    return lax.dot_general(a, b, dims, preferred_element_type=F32)


def split(a):
    high = a.astype(BF16)
    return high, (a - high.astype(F32)).astype(BF16)


def dot3(a, b, dims):
    return dot(a[0], b[0], dims) + (dot(a[0], b[1], dims) + dot(a[1], b[0], dims))


def greet(peers):
    barrier = pltpu.get_barrier_semaphore()
    for peer in peers:
        pl.semaphore_signal(barrier, inc=1, device_id=peer, device_id_type=MESH)
    pl.semaphore_wait(barrier, len(peers))


class Copies:
    def __init__(self, send_sem, recv_sem):
        self.send_sem, self.recv_sem, self.made = send_sem, recv_sem, []

    def send(self, src, dst, peer):
        i = len(self.made)
        copy = pltpu.make_async_remote_copy(
            src_ref=src,
            dst_ref=dst,
            send_sem=self.send_sem.at[i],
            recv_sem=self.recv_sem.at[i],
            device_id=peer,
            device_id_type=MESH,
        )
        copy.start()
        self.made.append(copy)
        return copy

    def finish(self):
        for copy in self.made:
            copy.wait_send()


def col_place():
    c = lax.axis_index("col")
    z, x = c // NX, c % NX
    along_x = [{"col": z * NX + (x + d) % NX} for d in range(1, NX)]
    along_z = [{"col": ((z + d) % NZ) * NX + x} for d in range(1, NZ)]
    return c, z, x, along_x, along_z


def gather_kernel(
    items, fetch, user, slot, er, ec, en, count, yh, yl, gram, ent, stage, land, send_sem, recv_sem, own_sem
):
    c, z, x, along_x, along_z = col_place()
    r = lax.axis_index("row")
    y, core = r // 2, r % 2
    right, left, across = (((y + d) % NY) * 2 + core for d in (1, 3, 2))
    other = y * 2 + 1 - core
    to_right, to_left, to_other = {"row": right}, {"row": left}, {"row": other}
    stage[0:TILES] = er[...]
    stage[TILES : 2 * TILES] = ec[...]
    stage[2 * TILES : 3 * TILES] = en[...]
    last = 3 * TILES
    stage[last : last + 1, 0:128] = fetch[...]
    stage[last + 1 : last + 2, 0:TILES] = slot[...]
    stage[last + 2 : last + 3, 0:TILES] = user[...]
    stage[last + 3 : last + 4, 0:128] = jnp.broadcast_to(count[...], (1, 128))
    own = pltpu.make_async_copy(stage, ent.at[z, x], own_sem)
    own.start()

    greet(along_x + along_z + [to_right, to_left, to_other])
    copies = Copies(send_sem, recv_sem)
    send = copies.send

    mine = [items.at[pl.ds(2 * i, 2)] for i in range(4)]
    there = [land.at[r, pl.ds(2 * i, 2)] for i in range(4)]
    from_left, from_right = {}, {}
    for i, j in zip((0, 1, 2, 3), (2, 3, 0, 1)):
        from_left[i] = send(mine[i], there[i], to_right)
        from_right[j] = send(mine[j], there[j], to_left)
    first, second = pl.ds(0, HALF), pl.ds(HALF, STAGE - HALF)
    by_x = [send(stage.at[first], ent.at[z, x, first], peer) for peer in along_x]
    by_z = [send(stage.at[second], ent.at[z, x, second], peer) for peer in along_z]
    between = [send(items, land.at[r], to_other)]
    own.wait()
    late = []
    for copy in by_x:
        copy.wait_recv()
    late += [send(ent.at[z, :, first], ent.at[z, :, first], peer) for peer in along_z]
    for copy in by_z:
        copy.wait_recv()
    late += [send(ent.at[:, x, second], ent.at[:, x, second], peer) for peer in along_x]
    far = []
    for i, j in ((0, 2), (1, 3)):
        from_left[i].wait_recv()
        piece = land.at[left, pl.ds(2 * i, 2)]
        far.append(send(piece, piece, to_right))
        from_right[j].wait_recv()
        piece = land.at[right, pl.ds(2 * j, 2)]
        far.append(send(piece, piece, to_left))
    for i, j in ((2, 0), (3, 1)):
        from_left[i].wait_recv()
        from_right[j].wait_recv()
    between.append(send(land.at[left], land.at[left], to_other))
    between.append(send(land.at[right], land.at[right], to_other))
    for copy in far:
        copy.wait_recv()
    between.append(send(land.at[across], land.at[across], to_other))
    for copy in between:
        copy.wait_recv()
    land[pl.ds(r, 1)] = items[...][None]

    def add(i, sums):
        high, low = split(land[i // IB, i % IB])
        yh[i] = high
        yl[i] = low
        return sums[0] + dot(high, high, TN), sums[1] + dot(high, low, TN)

    zero = jnp.zeros((K, K), F32)
    main, mixed = lax.fori_loop(0, ROWS * IB, add, (zero, zero))
    gram[...] = main + (mixed + mixed.T)
    for copy in late:
        copy.wait_recv()
    copies.finish()


def gather(items, fetch, user, slot, er, ec, en, count):
    n = 8 + 6 + 4 + 6 + 4
    return pl.pallas_call(
        gather_kernel,
        out_shape=(
            jax.ShapeDtypeStruct((ROWS * IB, BLOCK, K), BF16),
            jax.ShapeDtypeStruct((ROWS * IB, BLOCK, K), BF16),
            jax.ShapeDtypeStruct((K, K), F32),
            jax.ShapeDtypeStruct((NZ, NX, STAGE, NNZ), jnp.int32),
        ),
        in_specs=[VMEM] * 8,
        out_specs=(VMEM, VMEM, VMEM, ANY),
        scratch_shapes=[
            pltpu.VMEM((STAGE, NNZ), jnp.int32),
            pltpu.VMEM((ROWS, IB, BLOCK, K), F32),
            pltpu.SemaphoreType.DMA((n,)),
            pltpu.SemaphoreType.DMA((n,)),
            pltpu.SemaphoreType.DMA,
        ],
        compiler_params=pltpu.CompilerParams(
            collective_id=0, has_side_effects=True, vmem_limit_bytes=BIG
        ),
        name="gather",
    )(items, fetch, user, slot, er, ec, en, count)


def build_kernel(place, ent, yh, yl, gram, start, out, weights, order, meta, held, sem, meta_sem):
    fetched = pltpu.make_async_copy(
        ent.at[:, pl.ds(3 * TILES, 8), pl.ds(0, 128)], meta, meta_sem
    )
    fetched.start()
    g = split(gram[...])

    def begin(b, _):
        at = pl.ds(pl.multiple_of(b * BLOCK, BLOCK), BLOCK)
        out[at] = -dot3(split(start[at]), g, NN)
        return 0

    lax.fori_loop(0, UB, begin, 0)
    fetched.wait()
    me = place[0]

    def scan(c, n):
        def one(t, n):
            s = meta[c, 1, t]
            block = (s // COLS) * IB + meta[c, 0, s]
            order[n] = ((c * TILES + t) * 64 + block) * UB + meta[c, 2, t]
            return n + jnp.where(s % COLS == me, 1, 0)

        return lax.fori_loop(0, meta[c, 3, 0], one, n)

    n = lax.fori_loop(0, COLS, scan, 0)
    order[LIST - 1] = n
    ids = lax.broadcasted_iota(jnp.int32, (BLOCK, NNZ), 0)

    def out_copy(j):
        slot = j % 4
        return pltpu.make_async_copy(held.at[slot], weights.at[j], sem.at[slot])

    def tile(j, _):
        code = order[j]
        b, block, at = code % UB, (code // UB) % 64, code // (64 * UB)
        c, t = at // TILES, at % TILES
        rows = ent[c, pl.ds(t, 1), :]
        cols = ent[c, pl.ds(TILES + t, 1), :]
        counts = ent[c, pl.ds(2 * TILES + t, 1), :].astype(F32)
        row_hot = ids == rows
        col_hot = jnp.where(ids == cols, 1.0, 0.0).astype(BF16)
        ones = jnp.where(row_hot, 1.0, 0.0).astype(BF16)
        many = jnp.where(row_hot, counts, 0.0).astype(BF16)
        times = dot(ones, col_hot, NT)
        excess = SCALE * dot(many, col_hot, NT)

        @pl.when(j >= 4)
        def _():
            out_copy(j - 4).wait()

        held[j % 4] = excess
        out_copy(j).start()
        where = pl.ds(pl.multiple_of(b * BLOCK, BLOCK), BLOCK)
        item = (yh[block], yl[block])
        scores = dot3(split(start[where]), item, NT)
        pull = times + excess * (1.0 - scores)
        out[where] += dot3(split(pull), item, NN)
        return 0

    lax.fori_loop(0, n, tile, 0)

    def drain(j, _):
        out_copy(j).wait()
        return 0

    lax.fori_loop(jnp.maximum(n - 4, 0), n, drain, 0)


def build(place, ent, yh, yl, gram, start):
    return pl.pallas_call(
        build_kernel,
        out_shape=(
            jax.ShapeDtypeStruct((UB * BLOCK, K), F32),
            jax.ShapeDtypeStruct((ALL_TILES, BLOCK, BLOCK), F32),
            jax.ShapeDtypeStruct((LIST,), jnp.int32),
        ),
        in_specs=[SMEM] + [VMEM] * 5,
        out_specs=(VMEM, ANY, SMEM),
        scratch_shapes=[
            pltpu.SMEM((COLS, 8, 128), jnp.int32),
            pltpu.VMEM((4, BLOCK, BLOCK), F32),
            pltpu.SemaphoreType.DMA((4,)),
            pltpu.SemaphoreType.DMA,
        ],
        compiler_params=pltpu.CompilerParams(vmem_limit_bytes=BIG),
        name="build",
    )(place, ent, yh, yl, gram, start)


def each_tile(order, weights, held, sem, work):
    n = order[LIST - 1]

    def copy(base, i):
        return pltpu.make_async_copy(weights.at[base + i], held.at[i], sem.at[i])

    def batch(k, _):
        base = k * HELD
        here = jnp.minimum(n - base, HELD)

        def begin(i, _):
            copy(base, i).start()
            return 0

        lax.fori_loop(0, here, begin, 0)

        def group(q, _):
            for u in range(GROUP):
                i = q * GROUP + u

                @pl.when(i < here)
                def _(i=i):
                    copy(base, i).wait()

            for u in range(GROUP):
                i = q * GROUP + u
                live = i < here
                code = jnp.where(live, order[base + i], 0)
                w = jnp.where(live, held[i], 0.0)
                work(code % UB, (code // UB) % 64, w)
            return 0

        lax.fori_loop(0, (here + GROUP - 1) // GROUP, group, 0)
        return 0

    lax.fori_loop(0, (n + HELD - 1) // HELD, batch, 0)


def rows_of(b):
    return pl.ds(pl.multiple_of(b * BLOCK, BLOCK), BLOCK)


def dots(a, b):
    return jnp.sum(a * b, axis=1, keepdims=True)


def pull_tiles(order, weights, held, sem, yh, yl, vh, vl, out):
    def work(b, block, w):
        at = rows_of(b)
        item = (yh[block], yl[block])
        scores = dot3((vh[at], vl[at]), item, NT)
        out[at] += dot3(split(w * scores), item, NN)

    each_tile(order, weights, held, sem, work)


def first_kernel(order, total, start, yh, yl, gram, weights, out, residual, vh, vl, held, sem):
    g = split(gram[...])

    def begin(b, _):
        at = rows_of(b)
        v = total[at] - RIDGE * start[at]
        residual[at] = v
        high, low = split(v)
        vh[at], vl[at] = high, low
        out[at] = dot3((high, low), g, NN)
        return 0

    lax.fori_loop(0, UB, begin, 0)
    pull_tiles(order, weights, held, sem, yh, yl, vh, vl, out)


def update(total, iterate, residual, direction):
    image = total + RIDGE * direction
    now = dots(residual, residual)
    alpha = now / (dots(direction, image) + EPSILON)
    iterate = iterate + alpha * direction
    residual = residual - alpha * image
    after = dots(residual, residual)
    direction = residual + after / (now + EPSILON) * direction
    return iterate, residual, direction


def second_kernel(
    order, total, iterate, residual, yh, yl, gram, weights, out, new_x, new_r, new_p, vh, vl, held, sem
):
    g = split(gram[...])

    def begin(b, _):
        at = rows_of(b)
        r = residual[at]
        new_x[at], new_r[at], p = update(total[at], iterate[at], r, r)
        new_p[at] = p
        high, low = split(p)
        vh[at], vl[at] = high, low
        out[at] = dot3((high, low), g, NN)
        return 0

    lax.fori_loop(0, UB, begin, 0)
    pull_tiles(order, weights, held, sem, yh, yl, vh, vl, out)


def third_kernel(
    order, total, iterate, residual, direction, yh, yl, gram, weights,
    squares, new_x, new_r, new_p, vh, vl, acc, held, sem,
):
    g = split(gram[...])

    def begin(b, _):
        at = rows_of(b)
        new_x[at], new_r[at], p = update(total[at], iterate[at], residual[at], direction[at])
        new_p[at] = p
        high, low = split(p)
        vh[at], vl[at] = high, low
        acc[at] = p * dot3((high, low), g, NN)
        return 0

    lax.fori_loop(0, UB, begin, 0)

    def work(b, block, w):
        at = rows_of(b)
        scores = dot3((vh[at], vl[at]), (yh[block], yl[block]), NT)
        acc[at] += w * scores * scores

    each_tile(order, weights, held, sem, work)
    for b in range(UB):
        squares[b : b + 1] = jnp.sum(acc[b * BLOCK : (b + 1) * BLOCK].T, axis=0, keepdims=True)


def last_kernel(squares, iterate, residual, direction, out):
    sums = jnp.sum(squares[...], axis=0)
    for b in range(UB):
        at = pl.ds(b * BLOCK, BLOCK)
        p = direction[at]
        r = residual[at]
        below = jnp.broadcast_to(sums[b : b + 1], (BLOCK, BLOCK)).T + RIDGE * dots(p, p)
        out[at] = iterate[at] + dots(r, r) / (below + EPSILON) * p


USERS = jax.ShapeDtypeStruct((UB * BLOCK, K), F32)


def local(kernel, name, outs, specs, scratch=()):
    tiles = [
        pltpu.VMEM((UB * BLOCK, K), BF16),
        pltpu.VMEM((UB * BLOCK, K), BF16),
        *scratch,
        pltpu.VMEM((HELD, BLOCK, BLOCK), F32),
        pltpu.SemaphoreType.DMA((HELD,)),
    ]
    return pl.pallas_call(
        kernel,
        out_shape=outs,
        in_specs=specs,
        out_specs=tuple(VMEM for _ in outs),
        scratch_shapes=tiles,
        compiler_params=pltpu.CompilerParams(vmem_limit_bytes=BIG),
        name=name,
    )


def reduce_kernel(part, out, land_a, land_b, sum_a, sum_b, near_a, near_b, send_sem, recv_sem):
    c, z, x, along_x, along_z = col_place()
    greet(along_x + along_z)
    copies = Copies(send_sem, recv_sem)
    send = copies.send
    upper, lower = pl.ds(0, 64), pl.ds(64, 64)
    step_a = [
        send(part.at[:, (x + d) % NX, upper], land_a.at[d - 1], along_x[d - 1]) for d in (1, 2, 3)
    ]
    step_b = [
        send(part.at[(z + d) % NZ, :, lower], land_b.at[d - 1], along_z[d - 1]) for d in (1, 2, 3)
    ]
    for copy in step_a:
        copy.wait_recv()
    sum_a[...] = part[:, x, 0:64] + land_a[0] + (land_a[1] + land_a[2])
    next_a = [
        send(sum_a.at[(z + d) % NZ], near_a.at[d - 1], along_z[d - 1]) for d in (1, 2, 3)
    ]
    for copy in step_b:
        copy.wait_recv()
    sum_b[...] = part[z, :, 64:128] + land_b[0] + (land_b[1] + land_b[2])
    next_b = [
        send(sum_b.at[(x + d) % NX], near_b.at[d - 1], along_x[d - 1]) for d in (1, 2, 3)
    ]
    for copy in next_a:
        copy.wait_recv()
    out[z, x, 0:64] = sum_a[z] + near_a[0] + (near_a[1] + near_a[2])
    here = out.at[z, x, upper]
    back_a = [send(here, here, peer) for peer in along_z]
    for copy in next_b:
        copy.wait_recv()
    out[z, x, 64:128] = sum_b[x] + near_b[0] + (near_b[1] + near_b[2])
    here = out.at[z, x, lower]
    back_b = [send(here, here, peer) for peer in along_x]
    for copy in back_a:
        copy.wait_recv()
    line = out.at[:, x, upper]
    end = [send(line, line, peer) for peer in along_x]
    for copy in back_b:
        copy.wait_recv()
    line = out.at[z, :, lower]
    end += [send(line, line, peer) for peer in along_z]
    for copy in end:
        copy.wait_recv()
    copies.finish()


def reduce(part):
    out = pl.pallas_call(
        reduce_kernel,
        out_shape=jax.ShapeDtypeStruct((NZ, NX, BLOCK, K), F32),
        in_specs=[VMEM],
        out_specs=VMEM,
        scratch_shapes=[
            pltpu.VMEM((3, 4, 64, K), F32),
            pltpu.VMEM((3, 4, 64, K), F32),
            pltpu.VMEM((4, 64, K), F32),
            pltpu.VMEM((4, 64, K), F32),
            pltpu.VMEM((3, 64, K), F32),
            pltpu.VMEM((3, 64, K), F32),
            pltpu.SemaphoreType.DMA((24,)),
            pltpu.SemaphoreType.DMA((24,)),
        ],
        compiler_params=pltpu.CompilerParams(
            collective_id=1, has_side_effects=True, vmem_limit_bytes=BIG
        ),
        name="reduce",
    )(part.reshape(NZ, NX, BLOCK, K))
    return out.reshape(UB * BLOCK, K)


def scalars_kernel(mine, out, send_sem, recv_sem):
    c = lax.axis_index("col")
    peers = [{"col": (c + d) % COLS} for d in range(1, COLS)]
    greet(peers)
    copies = Copies(send_sem, recv_sem)
    made = [copies.send(mine, out.at[c], peer) for peer in peers]
    out[pl.ds(c, 1)] = mine[...][None]
    for copy in made:
        copy.wait_recv()
    copies.finish()


def gather_scalars(mine):
    return pl.pallas_call(
        scalars_kernel,
        out_shape=jax.ShapeDtypeStruct((COLS, UB, BLOCK), F32),
        in_specs=[VMEM],
        out_specs=VMEM,
        scratch_shapes=[
            pltpu.SemaphoreType.DMA((COLS - 1,)),
            pltpu.SemaphoreType.DMA((COLS - 1,)),
        ],
        compiler_params=pltpu.CompilerParams(collective_id=2, has_side_effects=True),
        name="scalars",
    )(mine)


def shards(user_factors, item_factors, fetch_list, tile_user, tile_slot, er, ec, en, tile_count):
    yh, yl, gram, ent = gather(
        item_factors.reshape(IB, BLOCK, K),
        fetch_list.reshape(1, 128),
        tile_user.reshape(1, TILES),
        tile_slot.reshape(1, TILES),
        er.reshape(TILES, NNZ),
        ec.reshape(TILES, NNZ),
        en.reshape(TILES, NNZ),
        tile_count.reshape(1, 1),
    )
    place = lax.axis_index("col").astype(jnp.int32).reshape(1)
    part, weights, order = build(
        place, ent.reshape(COLS, STAGE, NNZ), yh, yl, gram, user_factors
    )
    total = reduce(part)
    tail = [VMEM] * 3 + [ANY]
    part, residual = local(first_kernel, "first", (USERS,) * 2, [SMEM, VMEM, VMEM] + tail)(
        order, total, user_factors, yh, yl, gram, weights
    )
    total = reduce(part)
    part, iterate, residual, direction = local(
        second_kernel, "second", (USERS,) * 4, [SMEM] + [VMEM] * 3 + tail
    )(order, total, user_factors, residual, yh, yl, gram, weights)
    total = reduce(part)
    squares = jax.ShapeDtypeStruct((UB, BLOCK), F32)
    part, iterate, residual, direction = local(
        third_kernel,
        "third",
        (squares,) + (USERS,) * 3,
        [SMEM] + [VMEM] * 4 + tail,
        [pltpu.VMEM((UB * BLOCK, K), F32)],
    )(order, total, iterate, residual, direction, yh, yl, gram, weights)
    squares = gather_scalars(part)
    return pl.pallas_call(
        last_kernel,
        out_shape=USERS,
        in_specs=[VMEM] * 4,
        out_specs=VMEM,
        compiler_params=pltpu.CompilerParams(vmem_limit_bytes=BIG),
        name="last",
    )(squares, iterate, residual, direction)


def solution(mesh):
    return jax.shard_map(
        shards,
        mesh=mesh,
        in_specs=(
            P("row", None),
            P(("row", "col"), None),
            P("row", "col", None, None),
            P("row", "col", None),
            P("row", "col", None),
            P("row", "col", None, None),
            P("row", "col", None, None),
            P("row", "col", None, None),
            P("row", "col"),
        ),
        out_specs=P("row", None),
        check_vma=False,
    )
```

time: 702 us -> 209 us (0.30)
  the two profiles are of different devices: /device:TPU:0 before, /device:TPU:8 now
where the time goes in v1:
time: 209 us
  Pallas kernels  197 us (94%)
  local copies, waits for them, and re-layouts  11.3 us (5%)
    pallas_call x3, Pallas kernels, reduce(): pl.pallas_call(reduce_kernel, out_shape=jax.ShapeDtypeStruct((NZ, NX, BLO...  94.3 us
    pallas_call x1, Pallas kernels, gather(): pl.pallas_call(gather_kernel, out_shape=(jax.ShapeDtypeStruct((ROWS * IB,...  36.8 us
    pallas_call x1, Pallas kernels, build(): pl.pallas_call(build_kernel, out_shape=(jax.ShapeDtypeStruct((UB * BLOCK,...  18.2 us
    pallas_call x1, Pallas kernels, shards(): local(second_kernel, 'second', (USERS,) * 4, [SMEM] + [VMEM] * 3 + tail)  13 us
    pallas_call x1, Pallas kernels, gather_scalars(): pl.pallas_call(scalars_kernel, out_shape=jax.ShapeDtypeStruct((COLS, UB,...  11.6 us
    unnamed x32, local copies, waits for them, and re-layouts  11.3 us
    pallas_call x1, Pallas kernels, shards(): local(third_kernel, 'third', (squares,) + (USERS,) * 3, [SMEM] + [VMEM] *...  11 us
    pallas_call x1, Pallas kernels, shards(): local(first_kernel, 'first', (USERS,) * 2, [SMEM, VMEM, VMEM] + tail)  9.78 us

profile of v1, /device:TPU:8, one launch (start us, length us, event | category | flops | bytes accessed | tf_op | source)
XLA Modules:
  0.0 208.7 jit_solution(422086428483929351)
XLA Ops:
  0.7 0.0 copy-start.8
  0.7 1.0 copy-done.8
  1.7 0.0 copy-start.9
  1.7 0.8 copy-done.9
  2.5 0.0 copy-start.10
  2.5 0.8 copy-done.10
  3.4 0.0 copy-start.11
  3.4 0.8 copy-done.11
  4.2 0.0 copy-start.13
  4.2 0.7 copy-done.13
  4.9 0.0 copy-start.14
  4.9 0.7 copy-done.14
  5.5 0.0 copy-start.15
  5.5 0.7 copy-done.15
  6.2 36.8 %gather.1 = (bf16[64,128,128]{2,1,0:T(8,128)(2,1)S(1)}, bf16[64,128,128]{2,1,0:T(8,128)(2,1)S(1)}, f32[128,128]{1,0:T(8,128)S(1)}, s32[4,4,104,512]{3,2,1,0:T(8,128)}) custom-call(f32[8,128,128]{2,1,0:T(8,128)S(1)} %bitcast.21, s32[1,128]{1,0:T(1,128)S(1)} %bitcast.25, s32[1,32]{1,0:T(1,128)S(1)} %bitcast.26, s32[1,32]{1,0:T(1,128)S(1)} %bitcast.27, ...), custom_call_target="tpu_custom_call" | custom-call | tf_op jit(solution)/shard_map/gather/pallas_call | solution.py:170
  43.0 0.0 copy-start.1
  43.0 1.3 copy-done.1
  44.3 0.0 copy-start
  44.3 0.0 copy-start.2
  44.3 2.0 copy-done.2
  46.2 0.0 copy-start.3
  46.2 18.2 %build.1 = (f32[2048,128]{1,0:T(8,128)S(1)}, f32[512,128,128]{2,1,0:T(8,128)}, s32[1024]{0:T(1024)S(1)}) custom-call(s32[1]{0:T(128)} %bitcast.place, s32[16,104,512]{2,1,0:T(8,128)} %bitcast.28, bf16[64,128,128]{2,1,0:T(8,128)(2,1)S(1)} %get-tuple-element.23.yh, bf16[64,128,128]{2,1,0:T(8,128)(2,1)} %copy-done.1, f32[128,128]{1,0:T(8,128)S(1)} %get-tuple-element.25.gram, ...), custom_call_target="tpu_custom_call" | custom-call | tf_op jit(solution)/shard_map/build/pallas_call | solution.py:264
  64.5 0.0 copy-done
  64.5 33.0 %reduce.3 = f32[4,4,128,128]{3,2,1,0:T(8,128)S(1)} custom-call(f32[4,4,128,128]{3,2,1,0:T(8,128)S(1)} %bitcast.19), custom_call_target="tpu_custom_call" | custom-call | tf_op jit(solution)/shard_map/reduce/pallas_call | solution.py:493
  97.5 0.0 copy-done.3
  97.5 9.8 %first.1 = (f32[2048,128]{1,0:T(8,128)S(1)}, f32[2048,128]{1,0:T(8,128)S(1)}) custom-call(s32[1024]{0:T(1024)S(1)} %get-tuple-element.26.order, f32[2048,128]{1,0:T(8,128)S(1)} %bitcast.16, f32[2048,128]{1,0:T(8,128)S(1)} %copy-done.3, bf16[64,128,128]{2,1,0:T(8,128)(2,1)} %copy-done, bf16[64,128,128]{2,1,0:T(8,128)(2,1)} %copy-done.1, ...), custom_call_target="tpu_custom_call" | custom-call | tf_op jit(solution)/shard_map/first/pallas_call | solution.py:560
  107.3 0.0 copy-start.6
  107.3 32.5 %reduce.4 = f32[4,4,128,128]{3,2,1,0:T(8,128)S(1)} custom-call(f32[4,4,128,128]{3,2,1,0:T(8,128)S(1)} %bitcast.20), custom_call_target="tpu_custom_call" | custom-call | tf_op jit(solution)/shard_map/reduce/pallas_call | solution.py:493
  139.9 0.0 copy-done.6
  139.9 13.0 %second.1 = (f32[2048,128]{1,0:T(8,128)S(1)}, f32[2048,128]{1,0:T(8,128)S(1)}, f32[2048,128]{1,0:T(8,128)S(1)}, f32[2048,128]{1,0:T(8,128)S(1)}) custom-call(s32[1024]{0:T(1024)S(1)} %get-tuple-element.26.order, f32[2048,128]{1,0:T(8,128)S(1)} %bitcast.17, f32[2048,128]{1,0:T(8,128)} %iterate.1, f32[2048,128]{1,0:T(8,128)} %copy-done.6, ...), custom_call_target="tpu_custom_call" | custom-call | tf_op jit(solution)/shard_map/second/pallas_call | solution.py:564
  152.9 0.0 copy-start.4
  152.9 1.0 copy-done.4
  153.9 0.0 copy-start.5
  153.9 28.8 %reduce.5 = f32[4,4,128,128]{3,2,1,0:T(8,128)S(1)} custom-call(f32[4,4,128,128]{3,2,1,0:T(8,128)S(1)} %bitcast.18), custom_call_target="tpu_custom_call" | custom-call | tf_op jit(solution)/shard_map/reduce/pallas_call | solution.py:493
  182.7 0.0 copy-done.5
  182.7 11.0 %third.1 = (f32[16,128]{1,0:T(8,128)S(1)}, f32[2048,128]{1,0:T(8,128)S(1)}, f32[2048,128]{1,0:T(8,128)S(1)}, f32[2048,128]{1,0:T(8,128)S(1)}) custom-call(s32[1024]{0:T(1024)S(1)} %get-tuple-element.26.order, f32[2048,128]{1,0:T(8,128)S(1)} %bitcast.15, f32[2048,128]{1,0:T(8,128)S(1)} %get-tuple-element.32.iterate, f32[2048,128]{1,0:T(8,128)} %copy-done.4, ...), custom_call_target="tpu_custom_call" | custom-call | tf_op jit(solution)/shard_map/third/pallas_call | solution.py:569
  193.7 0.0 copy-start.12
  193.7 0.6 copy-done.12
  194.3 11.6 %scalars.1.squares = f32[16,16,128]{2,1,0:T(8,128)} custom-call(f32[16,128]{1,0:T(8,128)} %copy-done.12), custom_call_target="tpu_custom_call" | custom-call | tf_op jit(solution)/shard_map/scalars/pallas_call | solution.py:529
  205.9 0.0 copy-start.7
  205.9 0.9 copy-done.7
  206.8 1.9 last.1
Async XLA Ops:
  0.7 1.0 copy-start.8
  1.7 0.8 copy-start.9
  2.5 0.8 copy-start.10
  3.4 0.8 copy-start.11
  4.2 0.7 copy-start.13
  4.9 0.7 copy-start.14
  5.5 0.7 copy-start.15
  43.0 1.3 copy-start.1
  44.3 20.2 %copy-start = (bf16[64,128,128]{2,1,0:T(8,128)(2,1)}, bf16[64,128,128]{2,1,0:T(8,128)(2,1)S(1)}, u32[]{:S(2)}) copy-start(bf16[64,128,128]{2,1,0:T(8,128)(2,1)S(1)} %get-tuple-element.23.yh) | copy-start | bytes 6291460
  44.3 2.0 copy-start.2
  46.2 51.3 %copy-start.3 = (f32[2048,128]{1,0:T(8,128)S(1)}, f32[2048,128]{1,0:T(8,128)}, u32[]{:S(2)}) copy-start(f32[2048,128]{1,0:T(8,128)} %iterate.1) | copy-start | bytes 3145732
  107.3 32.6 %copy-start.6 = (f32[2048,128]{1,0:T(8,128)}, f32[2048,128]{1,0:T(8,128)S(1)}, u32[]{:S(2)}) copy-start(f32[2048,128]{1,0:T(8,128)S(1)} %get-tuple-element.30.residual) | copy-start | bytes 3145732
  152.9 1.0 copy-start.4
  153.9 28.8 %copy-start.5 = (f32[2048,128]{1,0:T(8,128)}, f32[2048,128]{1,0:T(8,128)S(1)}, u32[]{:S(2)}) copy-start(f32[2048,128]{1,0:T(8,128)S(1)} %get-tuple-element.34.direction) | copy-start | bytes 3145732
  193.7 0.6 copy-start.12
  205.9 0.9 copy-start.7

commit v2 on v1

v2 whole, which is shorter than its diff:
```python
import functools

import jax
import jax.numpy as jnp
from jax import lax
from jax.experimental import pallas as pl
from jax.experimental.pallas import tpu as pltpu
from jax.sharding import PartitionSpec as P

K = 128
BLOCK = 128
UB = 16
IB = 8
TILES = 32
NNZ = 512
NZ = NX = 4
NY = 4
ROWS = 8
COLS = 16
ALL_TILES = COLS * TILES
LIST = 1024
UNROLL = 4
BUILD = 4
SLOTS = 2 * BUILD
GROUP = 4
HELD = 32
STAGE = 3 * TILES + 8
HALF = 56
SCALE = 40.0
RIDGE = 0.5
EPSILON = 1e-06
MESH = pl.DeviceIdType.MESH
F32 = jnp.float32
BF16 = jnp.bfloat16
NT = (((1,), (1,)), ((), ()))
NN = (((1,), (0,)), ((), ()))
ANY = pl.BlockSpec(memory_space=pl.ANY)
VMEM = pl.BlockSpec(memory_space=pltpu.VMEM)
SMEM = pl.BlockSpec(memory_space=pltpu.SMEM)
BIG = 24 * 2**20


def dot(a, b, dims):
    return lax.dot_general(a, b, dims, preferred_element_type=F32)


def split(a):
    high = a.astype(BF16)
    return high, (a - high.astype(F32)).astype(BF16)


def pair(a):
    return jnp.concatenate(split(a), axis=1)


def fold(wide):
    return wide[:, 0:128] + wide[:, 128:256]


def by_cols(high, low):
    both = jnp.concatenate([high, low], axis=1)
    return jnp.concatenate([both, both], axis=0)


def greet(peers):
    barrier = pltpu.get_barrier_semaphore()
    for peer in peers:
        pl.semaphore_signal(barrier, inc=1, device_id=peer, device_id_type=MESH)
    pl.semaphore_wait(barrier, len(peers))


class Copies:
    def __init__(self, send_sem, recv_sem):
        self.send_sem, self.recv_sem, self.made = send_sem, recv_sem, []

    def send(self, src, dst, peer):
        i = len(self.made)
        copy = pltpu.make_async_remote_copy(
            src_ref=src,
            dst_ref=dst,
            send_sem=self.send_sem.at[i],
            recv_sem=self.recv_sem.at[i],
            device_id=peer,
            device_id_type=MESH,
        )
        copy.start()
        self.made.append(copy)
        return copy

    def finish(self):
        for copy in self.made:
            copy.wait_send()


def col_place():
    c = lax.axis_index("col")
    z, x = c // NX, c % NX
    along_x = [{"col": z * NX + (x + d) % NX} for d in range(1, NX)]
    along_z = [{"col": ((z + d) % NZ) * NX + x} for d in range(1, NZ)]
    return c, z, x, along_x, along_z


def gather_kernel(
    items, fetch, user, slot, er, ec, en, count, yh, yl, th, tl, gram, ent,
    stage, land, fetch_in, slot_in, user_in, small, send_sem, recv_sem, own_sem, in_sem,
):
    c, z, x, along_x, along_z = col_place()
    r = lax.axis_index("row")
    y, core = r // 2, r % 2
    right, left, across = (((y + d) % NY) * 2 + core for d in (1, 3, 2))
    other = y * 2 + 1 - core
    to_right, to_left, to_other = {"row": right}, {"row": left}, {"row": other}
    loads = [
        pltpu.make_async_copy(src, dst, in_sem.at[i])
        for i, (src, dst) in enumerate(
            (
                (er, stage.at[pl.ds(0, TILES)]),
                (ec, stage.at[pl.ds(TILES, TILES)]),
                (en, stage.at[pl.ds(2 * TILES, TILES)]),
                (items, land.at[r]),
                (fetch, fetch_in),
                (slot, slot_in),
                (user, user_in),
            )
        )
    ]
    for load in loads:
        load.start()
    greet(along_x + along_z + [to_right, to_left, to_other])
    copies = Copies(send_sem, recv_sem)
    send = copies.send

    half = [items.at[pl.ds(4 * i, 4)] for i in (0, 1)]
    there = [land.at[r, pl.ds(4 * i, 4)] for i in (0, 1)]
    from_left, from_right = [None, None], [None, None]
    for i in (0, 1):
        from_left[i] = send(half[i], there[i], to_right)
        from_right[1 - i] = send(half[1 - i], there[1 - i], to_left)
    between = [send(items, land.at[r], to_other)]

    for load in loads[4:]:
        load.wait()
    small[...] = jnp.zeros_like(small)
    small[0:1, 0:TILES] = slot_in[...]
    small[1:2, 0:TILES] = user_in[...]
    slots = small[0:1]
    table = jnp.broadcast_to(fetch_in[...].astype(F32), (128, 128)).T
    ids = lax.broadcasted_iota(jnp.int32, (128, 128), 0)
    local_id = jnp.sum(jnp.where(ids == slots, table, 0.0), axis=0, keepdims=True).astype(jnp.int32)
    lanes = lax.broadcasted_iota(jnp.int32, (1, 128), 1)
    last = 3 * TILES
    stage[last : last + 1, 0:128] = jnp.where(lanes < count[0, 0], slots & (COLS - 1), -1)
    stage[last + 1 : last + 2, 0:128] = ((slots >> 4) * IB + local_id) * UB + small[1:2]
    for load in loads[:3]:
        load.wait()
    own = pltpu.make_async_copy(stage, ent.at[z, x], own_sem)
    own.start()

    first, second = pl.ds(0, HALF), pl.ds(HALF, STAGE - HALF)
    parts = (pl.ds(0, 32), pl.ds(32, 24)), (pl.ds(56, 24), pl.ds(80, 24))
    ways = (
        (first, along_x, along_z, lambda d, e: ent.at[(z + e) % NZ, (x + d) % NX]),
        (second, along_z, along_x, lambda d, e: ent.at[(z + d) % NZ, (x + e) % NX]),
    )
    near = [[None] * 4, [None] * 4]
    up = [[None] * 4, [None] * 4]
    down = [[None] * 4, [None] * 4]

    def spread(w, d, source):
        rows, _, across_way, at = ways[w]
        to = at(-d, 0).at[rows]
        up[w][d] = send(source, to, across_way[0])
        down[w][d] = send(source, to, across_way[2])

    for w, (rows, along, _, at) in enumerate(ways):
        for d in (1, 3, 2):
            near[w][d] = send(stage.at[rows], at(0, 0).at[rows], along[d - 1])
        spread(w, 0, stage.at[rows])

    far = []

    def pass_on(w, d):
        _, _, across_way, at = ways[w]
        up[w][d].wait_recv()
        piece = at(-d, -1).at[parts[w][0]]
        far.append(send(piece, piece, across_way[0]))
        down[w][d].wait_recv()
        piece = at(-d, 1).at[parts[w][1]]
        far.append(send(piece, piece, across_way[2]))

    def add(row, sums):
        def one(i, sums):
            block = land[row, i]
            high, low = split(block)
            high_t, low_t = split(block.T)
            at = row * IB + i
            yh[at] = high
            yl[at] = low
            th[at] = high_t
            tl[at] = low_t
            return sums[0] + dot(high_t, high, NN), sums[1] + dot(high_t, low, NN)

        return lax.fori_loop(0, IB, one, sums, unroll=2)

    loads[3].wait()
    zero = jnp.zeros((K, K), F32)
    sums = add(r, (zero, zero))
    for d in (1, 3, 2):
        for w in (0, 1):
            near[w][d].wait_recv()
            rows, _, _, at = ways[w]
            spread(w, d, at(-d, 0).at[rows])
    for w in (0, 1):
        pass_on(w, 0)
    from_left[0].wait_recv()
    piece = land.at[left, pl.ds(0, 4)]
    round_y = [send(piece, piece, to_right)]
    from_right[1].wait_recv()
    piece = land.at[right, pl.ds(4, 4)]
    round_y.append(send(piece, piece, to_left))
    between[0].wait_recv()
    sums = add(other, sums)
    for d in (1, 3):
        for w in (0, 1):
            pass_on(w, d)
    from_left[1].wait_recv()
    between.append(send(land.at[left], land.at[left], to_other))
    from_right[0].wait_recv()
    between.append(send(land.at[right], land.at[right], to_other))
    for w in (0, 1):
        pass_on(w, 2)
    sums = add(left, sums)
    sums = add(right, sums)
    for copy in round_y:
        copy.wait_recv()
    between.append(send(land.at[across], land.at[across], to_other))
    sums = add(across, sums)
    for copy, d in zip(between[1:], (3, 1, 2)):
        copy.wait_recv()
        sums = add(((y + d) % NY) * 2 + 1 - core, sums)
    gram[...] = sums[0] + (sums[1] + sums[1].T)
    own.wait()
    for copy in far:
        copy.wait_recv()
    copies.finish()


def gather(items, fetch, user, slot, er, ec, en, count):
    n = 6 + 4 + 2 * (3 + 8 + 8)
    return pl.pallas_call(
        gather_kernel,
        out_shape=(
            *[jax.ShapeDtypeStruct((ROWS * IB, BLOCK, K), BF16)] * 4,
            jax.ShapeDtypeStruct((K, K), F32),
            jax.ShapeDtypeStruct((NZ, NX, STAGE, NNZ), jnp.int32),
        ),
        in_specs=[ANY] * 7 + [SMEM],
        out_specs=(VMEM, VMEM, VMEM, VMEM, VMEM, ANY),
        scratch_shapes=[
            pltpu.VMEM((STAGE, NNZ), jnp.int32),
            pltpu.VMEM((ROWS, IB, BLOCK, K), F32),
            pltpu.VMEM((1, 128), jnp.int32),
            pltpu.VMEM((1, TILES), jnp.int32),
            pltpu.VMEM((1, TILES), jnp.int32),
            pltpu.VMEM((8, 128), jnp.int32),
            pltpu.SemaphoreType.DMA((n,)),
            pltpu.SemaphoreType.DMA((n,)),
            pltpu.SemaphoreType.DMA,
            pltpu.SemaphoreType.DMA((7,)),
        ],
        compiler_params=pltpu.CompilerParams(
            collective_id=0, has_side_effects=True, vmem_limit_bytes=BIG
        ),
        name="gather",
    )(items, fetch, user, slot, er, ec, en, count)


def build_kernel(
    ent, yh, yl, th, tl, gram, start, out, weights, order, meta, held, v, sem, meta_sem
):
    fetched = pltpu.make_async_copy(
        ent.at[:, pl.ds(3 * TILES, 8), pl.ds(0, 128)], meta, meta_sem
    )
    fetched.start()
    g = by_cols(*split(gram[...]))

    def begin(b, _):
        at = rows_of(b)
        both = pair(start[at])
        v[at] = both
        out[at] = -fold(dot(both, g, NN))
        return 0

    lax.fori_loop(0, UB, begin, 0, unroll=UNROLL)
    fetched.wait()
    me = lax.axis_index("col")

    def scan(c, n):
        for t in range(TILES):
            order[n] = (c * TILES + t) * (64 * UB) + meta[c, 1, t]
            n = n + jnp.where(meta[c, 0, t] == me, 1, 0)
        return n

    n = lax.fori_loop(0, COLS, scan, 0)
    order[LIST - 1] = n
    ids = lax.broadcasted_iota(jnp.int32, (BLOCK, NNZ), 0).astype(F32).astype(BF16)
    one, none = jnp.ones((), BF16), jnp.zeros((), BF16)

    def out_copy(j):
        slot = j % SLOTS
        return pltpu.make_async_copy(held.at[slot], weights.at[j], sem.at[slot])

    def group(q, _):
        for u in range(BUILD):
            j = q * BUILD + u

            @pl.when((j >= SLOTS) & (j - SLOTS < n))
            def _(j=j):
                out_copy(j - SLOTS).wait()

        for u in range(BUILD):
            j = q * BUILD + u
            code = jnp.where(j < n, order[j], 0)
            b, block, at = code % UB, (code // UB) % 64, code // (64 * UB)
            c, t = at // TILES, at % TILES
            rows = jnp.where(j < n, ent[c, pl.ds(t, 1), :], BLOCK).astype(F32).astype(BF16)
            cols = ent[c, pl.ds(TILES + t, 1), :].astype(F32).astype(BF16)
            counts = ent[c, pl.ds(2 * TILES + t, 1), :].astype(F32).astype(BF16)
            row_hot = ids == rows
            col_hot = jnp.where(ids == cols, one, none)
            ones = jnp.where(row_hot, one, none)
            many = jnp.where(row_hot, counts, none)
            both = dot(jnp.concatenate([ones, many], axis=0), col_hot, NT)
            excess = SCALE * both[BLOCK:]
            held[j % SLOTS] = excess
            where = rows_of(b)
            scores = fold(dot(v[where], by_cols(th[block], tl[block]), NN))
            pull = both[:BLOCK] + excess * (1.0 - scores)
            out[where] += fold(dot(pair(pull), by_cols(yh[block], yl[block]), NN))
        for u in range(BUILD):
            j = q * BUILD + u

            @pl.when(j < n)
            def _(j=j):
                out_copy(j).start()

        return 0

    groups = (n + BUILD - 1) // BUILD
    lax.fori_loop(0, groups, group, 0)

    def drain(j, _):
        out_copy(j).wait()
        return 0

    lax.fori_loop(jnp.maximum(groups * BUILD - SLOTS, 0), n, drain, 0)


def build(ent, yh, yl, th, tl, gram, start):
    return pl.pallas_call(
        build_kernel,
        out_shape=(
            jax.ShapeDtypeStruct((UB * BLOCK, K), F32),
            jax.ShapeDtypeStruct((ALL_TILES, BLOCK, BLOCK), F32),
            jax.ShapeDtypeStruct((LIST,), jnp.int32),
        ),
        in_specs=[VMEM] * 7,
        out_specs=(VMEM, ANY, SMEM),
        scratch_shapes=[
            pltpu.SMEM((COLS, 8, 128), jnp.int32),
            pltpu.VMEM((SLOTS, BLOCK, BLOCK), F32),
            pltpu.VMEM((UB * BLOCK, 2 * K), BF16),
            pltpu.SemaphoreType.DMA((SLOTS,)),
            pltpu.SemaphoreType.DMA,
        ],
        compiler_params=pltpu.CompilerParams(vmem_limit_bytes=BIG),
        name="build",
    )(ent, yh, yl, th, tl, gram, start)


def fetch_tiles(order, weights, held, sem, base):
    here = jnp.minimum(order[LIST - 1] - base, HELD)

    def begin(i, _):
        pltpu.make_async_copy(weights.at[base + i], held.at[i], sem.at[i]).start()
        return 0

    lax.fori_loop(0, here, begin, 0)
    return here


def each_tile(order, weights, held, sem, work):
    n = order[LIST - 1]

    def batch(k, _):
        base = k * HELD
        here = jnp.minimum(n - base, HELD)

        def group(q, _):
            for u in range(GROUP):
                i = q * GROUP + u

                @pl.when(i < here)
                def _(i=i):
                    pltpu.make_async_copy(weights.at[base + i], held.at[i], sem.at[i]).wait()

            for u in range(GROUP):
                i = q * GROUP + u
                live = i < here
                code = jnp.where(live, order[base + i], 0)
                w = jnp.where(live, held[i], 0.0)
                work(code % UB, (code // UB) % 64, w)
            return 0

        lax.fori_loop(0, (here + GROUP - 1) // GROUP, group, 0)

        @pl.when(n > base + HELD)
        def _():
            fetch_tiles(order, weights, held, sem, base + HELD)

        return 0

    lax.fori_loop(0, (n + HELD - 1) // HELD, batch, 0)


def rows_of(b):
    return pl.ds(pl.multiple_of(b * BLOCK, BLOCK), BLOCK)


def dots(a, b):
    return jnp.sum(a * b, axis=1, keepdims=True)


def pull_tiles(order, weights, held, sem, yh, yl, th, tl, v, out):
    def work(b, block, w):
        at = rows_of(b)
        scores = fold(dot(v[at], by_cols(th[block], tl[block]), NN))
        out[at] += fold(dot(pair(w * scores), by_cols(yh[block], yl[block]), NN))

    each_tile(order, weights, held, sem, work)


def first_kernel(order, total, start, yh, yl, th, tl, gram, weights, out, residual, v, held, sem):
    fetch_tiles(order, weights, held, sem, 0)
    g = by_cols(*split(gram[...]))

    def begin(b, _):
        at = rows_of(b)
        p = total[at] - RIDGE * start[at]
        residual[at] = p
        both = pair(p)
        v[at] = both
        out[at] = fold(dot(both, g, NN))
        return 0

    lax.fori_loop(0, UB, begin, 0, unroll=UNROLL)
    pull_tiles(order, weights, held, sem, yh, yl, th, tl, v, out)


def update(total, iterate, residual, direction):
    image = total + RIDGE * direction
    now = dots(residual, residual)
    alpha = now / (dots(direction, image) + EPSILON)
    iterate = iterate + alpha * direction
    residual = residual - alpha * image
    after = dots(residual, residual)
    direction = residual + after / (now + EPSILON) * direction
    return iterate, residual, direction


def second_kernel(
    order, total, iterate, residual, yh, yl, th, tl, gram, weights, out, new_x, new_r, new_p, v, held, sem
):
    fetch_tiles(order, weights, held, sem, 0)
    g = by_cols(*split(gram[...]))

    def begin(b, _):
        at = rows_of(b)
        r = residual[at]
        new_x[at], new_r[at], p = update(total[at], iterate[at], r, r)
        new_p[at] = p
        both = pair(p)
        v[at] = both
        out[at] = fold(dot(both, g, NN))
        return 0

    lax.fori_loop(0, UB, begin, 0, unroll=UNROLL)
    pull_tiles(order, weights, held, sem, yh, yl, th, tl, v, out)


def third_kernel(
    order, total, iterate, residual, direction, yh, yl, th, tl, gram, weights,
    squares, new_x, new_r, new_p, v, acc, held, sem,
):
    fetch_tiles(order, weights, held, sem, 0)
    g = by_cols(*split(gram[...]))

    def begin(b, _):
        at = rows_of(b)
        new_x[at], new_r[at], p = update(total[at], iterate[at], residual[at], direction[at])
        new_p[at] = p
        both = pair(p)
        v[at] = both
        acc[at] = p * fold(dot(both, g, NN))
        return 0

    lax.fori_loop(0, UB, begin, 0, unroll=UNROLL)

    def work(b, block, w):
        at = rows_of(b)
        scores = fold(dot(v[at], by_cols(th[block], tl[block]), NN))
        acc[at] += w * scores * scores

    each_tile(order, weights, held, sem, work)
    for b in range(UB):
        squares[b : b + 1] = jnp.sum(acc[b * BLOCK : (b + 1) * BLOCK].T, axis=0, keepdims=True)


def last_kernel(squares, iterate, residual, direction, out):
    sums = squares[...]
    for b in range(UB):
        at = pl.ds(b * BLOCK, BLOCK)
        p = direction[at]
        r = residual[at]
        below = jnp.broadcast_to(sums[b : b + 1], (BLOCK, BLOCK)).T + RIDGE * dots(p, p)
        out[at] = iterate[at] + dots(r, r) / (below + EPSILON) * p


USERS = jax.ShapeDtypeStruct((UB * BLOCK, K), F32)


def local(kernel, name, outs, specs, scratch=()):
    tiles = [
        pltpu.VMEM((UB * BLOCK, 2 * K), BF16),
        *scratch,
        pltpu.VMEM((HELD, BLOCK, BLOCK), F32),
        pltpu.SemaphoreType.DMA((HELD,)),
    ]
    return pl.pallas_call(
        kernel,
        out_shape=outs,
        in_specs=specs,
        out_specs=tuple(VMEM for _ in outs),
        scratch_shapes=tiles,
        compiler_params=pltpu.CompilerParams(vmem_limit_bytes=BIG),
        name=name,
    )


def reduce_kernel(part, out, land_a, land_b, sum_a, sum_b, near_a, near_b, send_sem, recv_sem):
    c, z, x, along_x, along_z = col_place()
    greet(along_x + along_z)
    copies = Copies(send_sem, recv_sem)
    send = copies.send
    upper, lower = pl.ds(0, 64), pl.ds(64, 64)
    step_a = [
        send(part.at[:, (x + d) % NX, upper], land_a.at[d - 1], along_x[d - 1]) for d in (1, 2, 3)
    ]
    step_b = [
        send(part.at[(z + d) % NZ, :, lower], land_b.at[d - 1], along_z[d - 1]) for d in (1, 2, 3)
    ]
    for copy in step_a:
        copy.wait_recv()
    sum_a[...] = part[:, x, 0:64] + land_a[0] + (land_a[1] + land_a[2])
    next_a = [
        send(sum_a.at[(z + d) % NZ], near_a.at[d - 1], along_z[d - 1]) for d in (1, 2, 3)
    ]
    for copy in step_b:
        copy.wait_recv()
    sum_b[...] = part[z, :, 64:128] + land_b[0] + (land_b[1] + land_b[2])
    next_b = [
        send(sum_b.at[(x + d) % NX], near_b.at[d - 1], along_x[d - 1]) for d in (1, 2, 3)
    ]
    for copy in next_a:
        copy.wait_recv()
    out[z, x, 0:64] = sum_a[z] + near_a[0] + (near_a[1] + near_a[2])
    here = out.at[z, x, upper]
    back_a = [send(here, here, peer) for peer in along_z]
    for copy in next_b:
        copy.wait_recv()
    out[z, x, 64:128] = sum_b[x] + near_b[0] + (near_b[1] + near_b[2])
    here = out.at[z, x, lower]
    back_b = [send(here, here, peer) for peer in along_x]
    for copy in back_a:
        copy.wait_recv()
    line = out.at[:, x, upper]
    end = [send(line, line, peer) for peer in along_x]
    for copy in back_b:
        copy.wait_recv()
    line = out.at[z, :, lower]
    end += [send(line, line, peer) for peer in along_z]
    for copy in end:
        copy.wait_recv()
    copies.finish()


def reduce(part):
    out = pl.pallas_call(
        reduce_kernel,
        out_shape=jax.ShapeDtypeStruct((NZ, NX, BLOCK, K), F32),
        in_specs=[VMEM],
        out_specs=VMEM,
        scratch_shapes=[
            pltpu.VMEM((3, 4, 64, K), F32),
            pltpu.VMEM((3, 4, 64, K), F32),
            pltpu.VMEM((4, 64, K), F32),
            pltpu.VMEM((4, 64, K), F32),
            pltpu.VMEM((3, 64, K), F32),
            pltpu.VMEM((3, 64, K), F32),
            pltpu.SemaphoreType.DMA((24,)),
            pltpu.SemaphoreType.DMA((24,)),
        ],
        compiler_params=pltpu.CompilerParams(
            collective_id=1, has_side_effects=True, vmem_limit_bytes=BIG
        ),
        name="reduce",
    )(part.reshape(NZ, NX, BLOCK, K))
    return out.reshape(UB * BLOCK, K)


def scalars_kernel(mine, out, land_x, land_z, half, send_sem, recv_sem):
    _, _, _, along_x, along_z = col_place()
    greet(along_x + along_z)
    copies = Copies(send_sem, recv_sem)
    for copy in [copies.send(mine, land_x.at[i], peer) for i, peer in enumerate(along_x)]:
        copy.wait_recv()
    half[...] = mine[...] + land_x[0] + (land_x[1] + land_x[2])
    for copy in [copies.send(half, land_z.at[i], peer) for i, peer in enumerate(along_z)]:
        copy.wait_recv()
    out[...] = half[...] + land_z[0] + (land_z[1] + land_z[2])
    copies.finish()


def sum_scalars(mine):
    return pl.pallas_call(
        scalars_kernel,
        out_shape=jax.ShapeDtypeStruct((UB, BLOCK), F32),
        in_specs=[VMEM],
        out_specs=VMEM,
        scratch_shapes=[
            pltpu.VMEM((3, UB, BLOCK), F32),
            pltpu.VMEM((3, UB, BLOCK), F32),
            pltpu.VMEM((UB, BLOCK), F32),
            pltpu.SemaphoreType.DMA((6,)),
            pltpu.SemaphoreType.DMA((6,)),
        ],
        compiler_params=pltpu.CompilerParams(collective_id=2, has_side_effects=True),
        name="scalars",
    )(mine)


def shards(user_factors, item_factors, fetch_list, tile_user, tile_slot, er, ec, en, tile_count):
    yh, yl, th, tl, gram, ent = gather(
        item_factors.reshape(IB, BLOCK, K),
        fetch_list.reshape(1, 128),
        tile_user.reshape(1, TILES),
        tile_slot.reshape(1, TILES),
        er.reshape(TILES, NNZ),
        ec.reshape(TILES, NNZ),
        en.reshape(TILES, NNZ),
        tile_count.reshape(1, 1),
    )
    part, weights, order = build(
        ent.reshape(COLS, STAGE, NNZ), yh, yl, th, tl, gram, user_factors
    )
    total = reduce(part)
    tail = [VMEM] * 5 + [ANY]
    part, residual = local(first_kernel, "first", (USERS,) * 2, [SMEM, VMEM, VMEM] + tail)(
        order, total, user_factors, yh, yl, th, tl, gram, weights
    )
    total = reduce(part)
    part, iterate, residual, direction = local(
        second_kernel, "second", (USERS,) * 4, [SMEM] + [VMEM] * 3 + tail
    )(order, total, user_factors, residual, yh, yl, th, tl, gram, weights)
    total = reduce(part)
    squares = jax.ShapeDtypeStruct((UB, BLOCK), F32)
    part, iterate, residual, direction = local(
        third_kernel,
        "third",
        (squares,) + (USERS,) * 3,
        [SMEM] + [VMEM] * 4 + tail,
        [pltpu.VMEM((UB * BLOCK, K), F32)],
    )(order, total, iterate, residual, direction, yh, yl, th, tl, gram, weights)
    squares = sum_scalars(part)
    return pl.pallas_call(
        last_kernel,
        out_shape=USERS,
        in_specs=[VMEM] * 4,
        out_specs=VMEM,
        compiler_params=pltpu.CompilerParams(vmem_limit_bytes=BIG),
        name="last",
    )(squares, iterate, residual, direction)


def solution(mesh):
    return jax.shard_map(
        shards,
        mesh=mesh,
        in_specs=(
            P("row", None),
            P(("row", "col"), None),
            P("row", "col", None, None),
            P("row", "col", None),
            P("row", "col", None),
            P("row", "col", None, None),
            P("row", "col", None, None),
            P("row", "col", None, None),
            P("row", "col"),
        ),
        out_specs=P("row", None),
        check_vma=False,
    )
```

time: 209 us -> 154 us (0.74)
  Pallas kernels: 197 us -> 145 us
  local copies, waits for them, and re-layouts: 11.3 us -> 8.03 us
    pallas_call x3, Pallas kernels: 94.3 us -> 78.8 us  [reduce(): pl.pallas_call(reduce_kernel, out_shape=jax.ShapeDtypeStruct((NZ, NX, BLO...]
    pallas_call x1, Pallas kernels: 18.2 us -> 9.61 us  [build(): pl.pallas_call(build_kernel, out_shape=(jax.ShapeDtypeStruct((UB * BLOCK,...]
    pallas_call x1, Pallas kernels: 13 us -> 4.54 us  [shards(): local(second_kernel, 'second', (USERS,) * 4, [SMEM] + [VMEM] * 3 + tail)]
    pallas_call x1, Pallas kernels: 11 us -> 4.32 us  [shards(): local(third_kernel, 'third', (squares,) + (USERS,) * 3, [SMEM] + [VMEM] *...]
    pallas_call x2, Pallas kernels: 48.4 us -> 42.3 us  [the longest x1 31.4 us: gather(): pl.pallas_call(gather_kernel, out_shape=(*[jax.ShapeDtypeStruct((ROWS * I...]
    pallas_call x1, Pallas kernels: 9.78 us -> 3.69 us  [shards(): local(first_kernel, 'first', (USERS,) * 2, [SMEM, VMEM, VMEM] + tail)]
    unnamed x32 -> x22, local copies, waits for them, and re-layouts: 11.3 us -> 8.03 us
where the time goes in v2:
time: 154 us
  Pallas kernels  145 us (94%)
  local copies, waits for them, and re-layouts  8.03 us (5%)
    pallas_call x3, Pallas kernels, reduce(): pl.pallas_call(reduce_kernel, out_shape=jax.ShapeDtypeStruct((NZ, NX, BLO...  78.8 us
    pallas_call x1, Pallas kernels, gather(): pl.pallas_call(gather_kernel, out_shape=(*[jax.ShapeDtypeStruct((ROWS * I...  31.4 us
    pallas_call x1, Pallas kernels, sum_scalars(): pl.pallas_call(scalars_kernel, out_shape=jax.ShapeDtypeStruct((UB, BLOCK)...  10.8 us
    pallas_call x1, Pallas kernels, build(): pl.pallas_call(build_kernel, out_shape=(jax.ShapeDtypeStruct((UB * BLOCK,...  9.61 us
    unnamed x22, local copies, waits for them, and re-layouts  8.03 us
    pallas_call x1, Pallas kernels, shards(): local(second_kernel, 'second', (USERS,) * 4, [SMEM] + [VMEM] * 3 + tail)  4.54 us
    pallas_call x1, Pallas kernels, shards(): local(third_kernel, 'third', (squares,) + (USERS,) * 3, [SMEM] + [VMEM] *...  4.32 us
    pallas_call x1, Pallas kernels, shards(): local(first_kernel, 'first', (USERS,) * 2, [SMEM, VMEM, VMEM] + tail)  3.69 us

profile of v2, /device:TPU:8, one launch (start us, length us, event | category | flops | bytes accessed | tf_op | source)
XLA Modules:
  0.0 153.9 jit_solution(13702061582990498431)
XLA Ops:
  0.7 0.0 copy-start.2
  0.7 1.0 copy-done.2
  1.7 0.0 copy-start.3
  1.7 0.8 copy-done.3
  2.5 0.0 copy-start.4
  2.5 0.8 copy-done.4
  3.4 0.0 copy-start.5
  3.4 0.8 copy-done.5
  4.2 0.0 copy-start.8
  4.2 0.7 copy-done.8
  4.9 0.0 copy-start.9
  4.9 0.7 copy-done.9
  5.5 0.0 copy-start.10
  5.5 0.7 copy-done.10
  6.2 31.4 %gather.1 = (bf16[64,128,128]{2,1,0:T(8,128)(2,1)S(1)}, bf16[64,128,128]{2,1,0:T(8,128)(2,1)S(1)}, bf16[64,128,128]{2,1,0:T(8,128)(2,1)S(1)}, bf16[64,128,128]{2...) custom-call(f32[8,128,128]{2,1,0:T(8,128)S(1)} %bitcast.21, s32[1,128]{1,0:T(1,128)S(1)} %bitcast.25, ...), custom_call_target="tpu_custom_call" | custom-call | tf_op jit(solution)/shard_map/gather/pallas_call | solution.py:250
  37.6 0.0 copy-start
  37.6 1.2 copy-done
  38.9 9.6 %build.1 = (f32[2048,128]{1,0:T(8,128)S(1)}, f32[512,128,128]{2,1,0:T(8,128)}, s32[1024]{0:T(1024)S(1)}) custom-call(s32[16,104,512]{2,1,0:T(8,128)S(1)} %bitcast.17, bf16[64,128,128]{2,1,0:T(8,128)(2,1)S(1)} %get-tuple-element.25.yh, bf16[64,128,128]{2,1,0:T(8,128)(2,1)S(1)} %get-tuple-element.26.yl, bf16[64,128,128]{2,1,0:T(8,128)(2,1)S(1)} %get-tuple-element.27.th, ...), custom_call_target="tpu_custom_call" | custom-call | tf_op jit(solution)/shard_map/build/pallas_call | solution.py:360
  48.5 0.0 copy-start.1
  48.5 27.3 %reduce.3 = f32[4,4,128,128]{3,2,1,0:T(8,128)S(1)} custom-call(f32[4,4,128,128]{3,2,1,0:T(8,128)S(1)} %bitcast.19), custom_call_target="tpu_custom_call" | custom-call | tf_op jit(solution)/shard_map/reduce/pallas_call | solution.py:598
  75.8 0.0 copy-done.1
  75.8 3.7 %first.1 = (f32[2048,128]{1,0:T(8,128)S(1)}, f32[2048,128]{1,0:T(8,128)S(1)}) custom-call(s32[1024]{0:T(1024)S(1)} %get-tuple-element.30.order, f32[2048,128]{1,0:T(8,128)S(1)} %bitcast.16, f32[2048,128]{1,0:T(8,128)S(1)} %copy-done.1, bf16[64,128,128]{2,1,0:T(8,128)(2,1)S(1)} %get-tuple-element.25.yh, bf16[64,128,128]{2,1,0:T(8,128)(2,1)S(1)} %get-tuple-element.26.yl, ...), custom_call_target="tpu_custom_call" | custom-call | tf_op jit(solution)/shard_map/first/pallas_call | solution.py:668
  79.5 24.8 %reduce.4 = f32[4,4,128,128]{3,2,1,0:T(8,128)S(1)} custom-call(f32[4,4,128,128]{3,2,1,0:T(8,128)S(1)} %bitcast.20), custom_call_target="tpu_custom_call" | custom-call | tf_op jit(solution)/shard_map/reduce/pallas_call | solution.py:598
  104.4 4.5 %second.1 = (f32[2048,128]{1,0:T(8,128)S(1)}, f32[2048,128]{1,0:T(8,128)S(1)}, f32[2048,128]{1,0:T(8,128)S(1)}, f32[2048,128]{1,0:T(8,128)S(1)}) custom-call(s32[1024]{0:T(1024)S(1)} %get-tuple-element.30.order, f32[2048,128]{1,0:T(8,128)S(1)} %bitcast.15, f32[2048,128]{1,0:T(8,128)S(1)} %copy-done.1, f32[2048,128]{1,0:T(8,128)S(1)} %get-tuple-element.34.residual, ...), custom_call_target="tpu_custom_call" | custom-call | tf_op jit(solution)/shard_map/second/pallas_call | solution.py:672
  108.9 26.6 %reduce.5 = f32[4,4,128,128]{3,2,1,0:T(8,128)S(1)} custom-call(f32[4,4,128,128]{3,2,1,0:T(8,128)S(1)} %bitcast.18), custom_call_target="tpu_custom_call" | custom-call | tf_op jit(solution)/shard_map/reduce/pallas_call | solution.py:598
  135.5 4.3 %third.1 = (f32[16,128]{1,0:T(8,128)S(1)}, f32[2048,128]{1,0:T(8,128)S(1)}, f32[2048,128]{1,0:T(8,128)S(1)}, f32[2048,128]{1,0:T(8,128)S(1)}) custom-call(s32[1024]{0:T(1024)S(1)} %get-tuple-element.30.order, f32[2048,128]{1,0:T(8,128)S(1)} %bitcast.14, f32[2048,128]{1,0:T(8,128)S(1)} %get-tuple-element.36.iterate, ...), custom_call_target="tpu_custom_call" | custom-call | tf_op jit(solution)/shard_map/third/pallas_call | solution.py:677
  139.9 0.0 copy-start.7
  139.9 0.6 copy-done.7
  140.5 10.8 %scalars.1.squares = f32[16,128]{1,0:T(8,128)} custom-call(f32[16,128]{1,0:T(8,128)} %copy-done.7), custom_call_target="tpu_custom_call" | custom-call | tf_op jit(solution)/shard_map/scalars/pallas_call | solution.py:635
  151.3 0.0 copy-start.6
  151.3 0.7 copy-done.6
  152.0 1.9 %last.1 = f32[2048,128]{1,0:T(8,128)} custom-call(f32[16,128]{1,0:T(8,128)S(1)} %copy-done.6, f32[2048,128]{1,0:T(8,128)S(1)} %get-tuple-element.40.iterate, f32[2048,128]{1,0:T(8,128)S(1)} %get-tuple-element.41.residual, f32[2048,128]{1,0:T(8,128)S(1)} %get-tuple-element.42.direction), custom_call_target="tpu_custom_call" | custom-call | tf_op jit(solution)/shard_map/last/pallas_call | solution.py:685
Async XLA Ops:
  0.7 1.0 copy-start.2
  1.7 0.8 copy-start.3
  2.5 0.8 copy-start.4
  3.4 0.8 copy-start.5
  4.2 0.7 copy-start.8
  4.9 0.7 copy-start.9
  5.5 0.7 copy-start.10
  37.6 1.2 copy-start
  48.5 27.4 %copy-start.1 = (f32[2048,128]{1,0:T(8,128)S(1)}, f32[2048,128]{1,0:T(8,128)}, u32[]{:S(2)}) copy-start(f32[2048,128]{1,0:T(8,128)} %iterate.1) | copy-start | bytes 3145732
  139.9 0.6 copy-start.7
  151.3 0.7 copy-start.6

commit v3 on v2

--- a/solution.py
+++ b/solution.py
@@ -19,6 +19,7 @@
 COLS = 16
 ALL_TILES = COLS * TILES
 LIST = 1024
+SUB = 32
 UNROLL = 4
 BUILD = 4
 SLOTS = 2 * BUILD
@@ -37,6 +38,7 @@
 ANY = pl.BlockSpec(memory_space=pl.ANY)
 VMEM = pl.BlockSpec(memory_space=pltpu.VMEM)
 SMEM = pl.BlockSpec(memory_space=pltpu.SMEM)
+HBM = pl.BlockSpec(memory_space=pltpu.HBM)
 BIG = 24 * 2**20
 
 
@@ -190,21 +192,19 @@
 
     def add(row, sums):
         def one(i, sums):
-            block = land[row, i]
-            high, low = split(block)
-            high_t, low_t = split(block.T)
+            high, low = split(land[row, i])
+            high_t = high.T
             at = row * IB + i
             yh[at] = high
             yl[at] = low
             th[at] = high_t
-            tl[at] = low_t
-            return sums[0] + dot(high_t, high, NN), sums[1] + dot(high_t, low, NN)
-
-        return lax.fori_loop(0, IB, one, sums, unroll=2)
+            tl[at] = low.T
+            return sums + dot(high_t, jnp.concatenate([high, low], axis=1), NN)
+
+        return lax.fori_loop(0, IB, one, sums, unroll=4)
 
     loads[3].wait()
-    zero = jnp.zeros((K, K), F32)
-    sums = add(r, (zero, zero))
+    sums = add(r, jnp.zeros((K, 2 * K), F32))
     for d in (1, 3, 2):
         for w in (0, 1):
             near[w][d].wait_recv()
@@ -238,7 +238,8 @@
     for copy, d in zip(between[1:], (3, 1, 2)):
         copy.wait_recv()
         sums = add(((y + d) % NY) * 2 + 1 - core, sums)
-    gram[...] = sums[0] + (sums[1] + sums[1].T)
+    mixed = sums[:, K:]
+    gram[...] = sums[:, :K] + (mixed + mixed.T)
     own.wait()
     for copy in far:
         copy.wait_recv()
@@ -254,7 +255,7 @@
             jax.ShapeDtypeStruct((K, K), F32),
             jax.ShapeDtypeStruct((NZ, NX, STAGE, NNZ), jnp.int32),
         ),
-        in_specs=[ANY] * 7 + [SMEM],
+        in_specs=[HBM] * 7 + [SMEM],
         out_specs=(VMEM, VMEM, VMEM, VMEM, VMEM, ANY),
         scratch_shapes=[
             pltpu.VMEM((STAGE, NNZ), jnp.int32),
@@ -272,7 +273,7 @@
             collective_id=0, has_side_effects=True, vmem_limit_bytes=BIG
         ),
         name="gather",
-    )(items, fetch, user, slot, er, ec, en, count)
+    )(*[pltpu.with_memory_space_constraint(a, pltpu.HBM) for a in (items, fetch, user, slot, er, ec, en)], count)
 
 
 def build_kernel(
@@ -547,68 +548,65 @@
     )
 
 
-def reduce_kernel(part, out, land_a, land_b, sum_a, sum_b, near_a, near_b, send_sem, recv_sem):
+def reduce_kernel(part, out, land, sums, near, send_sem, recv_sem):
     c, z, x, along_x, along_z = col_place()
     greet(along_x + along_z)
     copies = Copies(send_sem, recv_sem)
     send = copies.send
-    upper, lower = pl.ds(0, 64), pl.ds(64, 64)
-    step_a = [
-        send(part.at[:, (x + d) % NX, upper], land_a.at[d - 1], along_x[d - 1]) for d in (1, 2, 3)
+    streams = [(pl.ds(SUB * i, SUB), i % 2 == 0) for i in range(BLOCK // SUB)]
+
+    def line(ref, way, d, rows):
+        return ref.at[:, (x + d) % NX, rows] if way else ref.at[(z + d) % NZ, :, rows]
+
+    def axes(way):
+        return (along_x, along_z, z) if way else (along_z, along_x, x)
+
+    far = [
+        [send(line(part, way, d, rows), land.at[i, d - 1], axes(way)[0][d - 1]) for d in (1, 2, 3)]
+        for i, (rows, way) in enumerate(streams)
     ]
-    step_b = [
-        send(part.at[(z + d) % NZ, :, lower], land_b.at[d - 1], along_z[d - 1]) for d in (1, 2, 3)
-    ]
-    for copy in step_a:
-        copy.wait_recv()
-    sum_a[...] = part[:, x, 0:64] + land_a[0] + (land_a[1] + land_a[2])
-    next_a = [
-        send(sum_a.at[(z + d) % NZ], near_a.at[d - 1], along_z[d - 1]) for d in (1, 2, 3)
-    ]
-    for copy in step_b:
-        copy.wait_recv()
-    sum_b[...] = part[z, :, 64:128] + land_b[0] + (land_b[1] + land_b[2])
-    next_b = [
-        send(sum_b.at[(x + d) % NX], near_b.at[d - 1], along_x[d - 1]) for d in (1, 2, 3)
-    ]
-    for copy in next_a:
-        copy.wait_recv()
-    out[z, x, 0:64] = sum_a[z] + near_a[0] + (near_a[1] + near_a[2])
-    here = out.at[z, x, upper]
-    back_a = [send(here, here, peer) for peer in along_z]
-    for copy in next_b:
-        copy.wait_recv()
-    out[z, x, 64:128] = sum_b[x] + near_b[0] + (near_b[1] + near_b[2])
-    here = out.at[z, x, lower]
-    back_b = [send(here, here, peer) for peer in along_x]
-    for copy in back_a:
-        copy.wait_recv()
-    line = out.at[:, x, upper]
-    end = [send(line, line, peer) for peer in along_x]
-    for copy in back_b:
-        copy.wait_recv()
-    line = out.at[z, :, lower]
-    end += [send(line, line, peer) for peer in along_z]
+    close = []
+    for i, (rows, way) in enumerate(streams):
+        _, along, me = axes(way)
+        for copy in far[i]:
+            copy.wait_recv()
+        mine = part[:, x, rows] if way else part[z, :, rows]
+        sums[i] = mine + land[i, 0] + (land[i, 1] + land[i, 2])
+        close.append(
+            [send(sums.at[i, (me + d) % 4], near.at[i, d - 1], along[d - 1]) for d in (1, 2, 3)]
+        )
+    back = []
+    for i, (rows, way) in enumerate(streams):
+        _, along, me = axes(way)
+        for copy in close[i]:
+            copy.wait_recv()
+        out[z, x, rows] = sums[i, me] + near[i, 0] + (near[i, 1] + near[i, 2])
+        here = out.at[z, x, rows]
+        back.append([send(here, here, peer) for peer in along])
+    end = []
+    for i, (rows, way) in enumerate(streams):
+        for copy in back[i]:
+            copy.wait_recv()
+        here = line(out, way, 0, rows)
+        end += [send(here, here, peer) for peer in axes(way)[0]]
     for copy in end:
         copy.wait_recv()
     copies.finish()
 
 
 def reduce(part):
+    n = BLOCK // SUB
     out = pl.pallas_call(
         reduce_kernel,
         out_shape=jax.ShapeDtypeStruct((NZ, NX, BLOCK, K), F32),
         in_specs=[VMEM],
         out_specs=VMEM,
         scratch_shapes=[
-            pltpu.VMEM((3, 4, 64, K), F32),
-            pltpu.VMEM((3, 4, 64, K), F32),
-            pltpu.VMEM((4, 64, K), F32),
-            pltpu.VMEM((4, 64, K), F32),
-            pltpu.VMEM((3, 64, K), F32),
-            pltpu.VMEM((3, 64, K), F32),
-            pltpu.SemaphoreType.DMA((24,)),
-            pltpu.SemaphoreType.DMA((24,)),
+            pltpu.VMEM((n, 3, 4, SUB, K), F32),
+            pltpu.VMEM((n, 4, SUB, K), F32),
+            pltpu.VMEM((n, 3, SUB, K), F32),
+            pltpu.SemaphoreType.DMA((12 * n,)),
+            pltpu.SemaphoreType.DMA((12 * n,)),
         ],
         compiler_params=pltpu.CompilerParams(
             collective_id=1, has_side_effects=True, vmem_limit_bytes=BIG
@@ -644,7 +642,7 @@
             pltpu.SemaphoreType.DMA((6,)),
             pltpu.SemaphoreType.DMA((6,)),
         ],
-        compiler_params=pltpu.CompilerParams(collective_id=2, has_side_effects=True),
+        compiler_params=pltpu.CompilerParams(collective_id=2, has_side_effects=True, vmem_limit_bytes=BIG),
         name="scalars",
     )(mine)
 

time: 154 us -> 139 us (0.903)
  the two profiles are of different devices: /device:TPU:8 before, /device:TPU:0 now
where the time goes in v3:
time: 139 us; the launch traced here: 137 us
  Pallas kernels  136 us (98%)
    pallas_call x3, Pallas kernels, reduce(): pl.pallas_call(reduce_kernel, out_shape=jax.ShapeDtypeStruct((NZ, NX, BLO...  72.9 us
    pallas_call x1, Pallas kernels, gather(): pl.pallas_call(gather_kernel, out_shape=(*[jax.ShapeDtypeStruct((ROWS * I...  29.3 us
    pallas_call x1, Pallas kernels, build(): pl.pallas_call(build_kernel, out_shape=(jax.ShapeDtypeStruct((UB * BLOCK,...  9.59 us
    pallas_call x1, Pallas kernels, sum_scalars(): pl.pallas_call(scalars_kernel, out_shape=jax.ShapeDtypeStruct((UB, BLOCK)...  9.25 us
    pallas_call x1, Pallas kernels, shards(): local(second_kernel, 'second', (USERS,) * 4, [SMEM] + [VMEM] * 3 + tail)  4.53 us
    pallas_call x1, Pallas kernels, shards(): local(third_kernel, 'third', (squares,) + (USERS,) * 3, [SMEM] + [VMEM] *...  4.31 us
    pallas_call x1, Pallas kernels, shards(): local(first_kernel, 'first', (USERS,) * 2, [SMEM, VMEM, VMEM] + tail)  3.68 us

profile of v3, /device:TPU:0, one launch (start us, length us, event | category | flops | bytes accessed | tf_op | source)
XLA Modules:
  0.0 137.5 jit_solution(599991791865917645)
XLA Ops:
  0.7 29.3 %gather.1 = (bf16[64,128,128]{2,1,0:T(8,128)(2,1)S(1)}, bf16[64,128,128]{2,1,0:T(8,128)(2,1)S(1)}, bf16[64,128,128]{2,1,0:T(8,128)(2,1)S(1)}, bf16[64,128,128]{2...) custom-call(f32[8,128,128]{2,1,0:T(8,128)} %bitcast.21, s32[1,128]{1,0:T(1,128)} %bitcast.25, ...), custom_call_target="tpu_custom_call" | custom-call | tf_op jit(solution)/shard_map/gather/pallas_call | solution.py:251
  30.0 0.0 copy-start
  30.0 1.2 copy-done
  31.2 9.6 %build.1 = (f32[2048,128]{1,0:T(8,128)S(1)}, f32[512,128,128]{2,1,0:T(8,128)}, s32[1024]{0:T(1024)S(1)}) custom-call(s32[16,104,512]{2,1,0:T(8,128)S(1)} %bitcast.17, bf16[64,128,128]{2,1,0:T(8,128)(2,1)S(1)} %get-tuple-element.25.yh, bf16[64,128,128]{2,1,0:T(8,128)(2,1)S(1)} %get-tuple-element.26.yl, bf16[64,128,128]{2,1,0:T(8,128)(2,1)S(1)} %get-tuple-element.27.th, ...), custom_call_target="tpu_custom_call" | custom-call | tf_op jit(solution)/shard_map/build/pallas_call | solution.py:361
  40.8 0.0 copy-start.1
  40.8 27.3 %reduce.3 = f32[4,4,128,128]{3,2,1,0:T(8,128)S(1)} custom-call(f32[4,4,128,128]{3,2,1,0:T(8,128)S(1)} %bitcast.19), custom_call_target="tpu_custom_call" | custom-call | tf_op jit(solution)/shard_map/reduce/pallas_call | solution.py:599
  68.1 0.0 copy-done.1
  68.1 3.7 %first.1 = (f32[2048,128]{1,0:T(8,128)S(1)}, f32[2048,128]{1,0:T(8,128)S(1)}) custom-call(s32[1024]{0:T(1024)S(1)} %get-tuple-element.30.order, f32[2048,128]{1,0:T(8,128)S(1)} %bitcast.16, f32[2048,128]{1,0:T(8,128)S(1)} %copy-done.1, bf16[64,128,128]{2,1,0:T(8,128)(2,1)S(1)} %get-tuple-element.25.yh, bf16[64,128,128]{2,1,0:T(8,128)(2,1)S(1)} %get-tuple-element.26.yl, ...), custom_call_target="tpu_custom_call" | custom-call | tf_op jit(solution)/shard_map/first/pallas_call | solution.py:666
  71.8 22.8 %reduce.4 = f32[4,4,128,128]{3,2,1,0:T(8,128)S(1)} custom-call(f32[4,4,128,128]{3,2,1,0:T(8,128)S(1)} %bitcast.20), custom_call_target="tpu_custom_call" | custom-call | tf_op jit(solution)/shard_map/reduce/pallas_call | solution.py:599
  94.6 4.5 %second.1 = (f32[2048,128]{1,0:T(8,128)S(1)}, f32[2048,128]{1,0:T(8,128)S(1)}, f32[2048,128]{1,0:T(8,128)S(1)}, f32[2048,128]{1,0:T(8,128)S(1)}) custom-call(s32[1024]{0:T(1024)S(1)} %get-tuple-element.30.order, f32[2048,128]{1,0:T(8,128)S(1)} %bitcast.15, f32[2048,128]{1,0:T(8,128)S(1)} %copy-done.1, f32[2048,128]{1,0:T(8,128)S(1)} %get-tuple-element.34.residual, ...), custom_call_target="tpu_custom_call" | custom-call | tf_op jit(solution)/shard_map/second/pallas_call | solution.py:670
  99.2 22.8 %reduce.5 = f32[4,4,128,128]{3,2,1,0:T(8,128)S(1)} custom-call(f32[4,4,128,128]{3,2,1,0:T(8,128)S(1)} %bitcast.18), custom_call_target="tpu_custom_call" | custom-call | tf_op jit(solution)/shard_map/reduce/pallas_call | solution.py:599
  122.0 4.3 %third.1 = (f32[16,128]{1,0:T(8,128)S(1)}, f32[2048,128]{1,0:T(8,128)S(1)}, f32[2048,128]{1,0:T(8,128)S(1)}, f32[2048,128]{1,0:T(8,128)S(1)}) custom-call(s32[1024]{0:T(1024)S(1)} %get-tuple-element.30.order, f32[2048,128]{1,0:T(8,128)S(1)} %bitcast.14, f32[2048,128]{1,0:T(8,128)S(1)} %get-tuple-element.36.iterate, ...), custom_call_target="tpu_custom_call" | custom-call | tf_op jit(solution)/shard_map/third/pallas_call | solution.py:675
  126.3 9.3 %scalars.1.squares = f32[16,128]{1,0:T(8,128)S(1)} custom-call(f32[16,128]{1,0:T(8,128)S(1)} %get-tuple-element.39.mine), custom_call_target="tpu_custom_call" | custom-call | tf_op jit(solution)/shard_map/scalars/pallas_call | solution.py:633
  135.6 1.9 %last.1 = f32[2048,128]{1,0:T(8,128)} custom-call(f32[16,128]{1,0:T(8,128)S(1)} %scalars.1.squares, f32[2048,128]{1,0:T(8,128)S(1)} %get-tuple-element.40.iterate, f32[2048,128]{1,0:T(8,128)S(1)} %get-tuple-element.41.residual, f32[2048,128]{1,0:T(8,128)S(1)} %get-tuple-element.42.direction), custom_call_target="tpu_custom_call" | custom-call | tf_op jit(solution)/shard_map/last/pallas_call | solution.py:683
Async XLA Ops:
  30.0 1.2 copy-start
  40.8 27.3 %copy-start.1 = (f32[2048,128]{1,0:T(8,128)S(1)}, f32[2048,128]{1,0:T(8,128)}, u32[]{:S(2)}) copy-start(f32[2048,128]{1,0:T(8,128)} %iterate.1) | copy-start | bytes 3145732

commit v4 on v3

--- a/solution.py
+++ b/solution.py
@@ -19,6 +19,10 @@
 COLS = 16
 ALL_TILES = COLS * TILES
 LIST = 1024
+LAST = 512
+FAST = 40
+QUARTER = 10
+STEP = 5
 SUB = 32
 UNROLL = 4
 BUILD = 4
@@ -40,6 +44,7 @@
 SMEM = pl.BlockSpec(memory_space=pltpu.SMEM)
 HBM = pl.BlockSpec(memory_space=pltpu.HBM)
 BIG = 24 * 2**20
+WHOLE = 40 * 2**20
 
 
 def dot(a, b, dims):
@@ -103,8 +108,8 @@
 
 
 def gather_kernel(
-    items, fetch, user, slot, er, ec, en, count, yh, yl, th, tl, gram, ent,
-    stage, land, fetch_in, slot_in, user_in, small, send_sem, recv_sem, own_sem, in_sem,
+    items, fetch, user, slot, er, ec, en, count, yh, yl, th, tl, gram, ent, peak,
+    stage, land, fetch_in, slot_in, user_in, small, keys, most, seen, send_sem, recv_sem, own_sem, in_sem,
 ):
     c, z, x, along_x, along_z = col_place()
     r = lax.axis_index("row")
@@ -231,32 +236,65 @@
         pass_on(w, 2)
     sums = add(left, sums)
     sums = add(right, sums)
+    for copy in far:
+        copy.wait_recv()
+    own.wait()
+    load = pltpu.make_async_copy(ent.at[:, :, pl.ds(last, 8), pl.ds(0, 128)], keys, own_sem)
+    load.start()
+    load.wait()
+
+    owners = keys[:, :, 0, :].reshape(COLS, 128)
+    longest = jnp.zeros((1, 1), jnp.int32)
+    for column in range(COLS):
+        here = jnp.where(owners == column, 1, 0)
+        here = jnp.sum(jnp.sum(here, axis=0, keepdims=True), axis=1, keepdims=True)
+        longest = jnp.maximum(longest, here)
+    most[0] = jnp.broadcast_to(longest, (8, 128))
+
+    def tell(i):
+        return [
+            send(most.at[i], seen.at[i, n], peer)
+            for n, peer in enumerate((to_right, to_left, to_other))
+        ]
+
+    def learn(i, told):
+        for copy in told:
+            copy.wait_recv()
+        most[i + 1] = jnp.maximum(
+            jnp.maximum(most[i], seen[i, 0]), jnp.maximum(seen[i, 1], seen[i, 2])
+        )
+
+    told = tell(0)
     for copy in round_y:
         copy.wait_recv()
     between.append(send(land.at[across], land.at[across], to_other))
+    learn(0, told)
+    told = tell(1)
     sums = add(across, sums)
+    learn(1, told)
+    told = tell(2)
     for copy, d in zip(between[1:], (3, 1, 2)):
         copy.wait_recv()
         sums = add(((y + d) % NY) * 2 + 1 - core, sums)
+    learn(2, told)
+    peak[...] = most[3]
     mixed = sums[:, K:]
     gram[...] = sums[:, :K] + (mixed + mixed.T)
-    own.wait()
-    for copy in far:
-        copy.wait_recv()
     copies.finish()
 
 
 def gather(items, fetch, user, slot, er, ec, en, count):
-    n = 6 + 4 + 2 * (3 + 8 + 8)
+    n = 6 + 4 + 2 * (3 + 8 + 8) + 9
     return pl.pallas_call(
         gather_kernel,
         out_shape=(
             *[jax.ShapeDtypeStruct((ROWS * IB, BLOCK, K), BF16)] * 4,
             jax.ShapeDtypeStruct((K, K), F32),
             jax.ShapeDtypeStruct((NZ, NX, STAGE, NNZ), jnp.int32),
+            jax.ShapeDtypeStruct((8, 128), jnp.int32),
         ),
         in_specs=[HBM] * 7 + [SMEM],
-        out_specs=(VMEM, VMEM, VMEM, VMEM, VMEM, ANY),
+        out_specs=(VMEM, VMEM, VMEM, VMEM, VMEM, ANY, VMEM),
         scratch_shapes=[
             pltpu.VMEM((STAGE, NNZ), jnp.int32),
             pltpu.VMEM((ROWS, IB, BLOCK, K), F32),
@@ -264,6 +302,9 @@
             pltpu.VMEM((1, TILES), jnp.int32),
             pltpu.VMEM((1, TILES), jnp.int32),
             pltpu.VMEM((8, 128), jnp.int32),
+            pltpu.VMEM((NZ, NX, 8, 128), jnp.int32),
+            pltpu.VMEM((4, 8, 128), jnp.int32),
+            pltpu.VMEM((3, 3, 8, 128), jnp.int32),
             pltpu.SemaphoreType.DMA((n,)),
             pltpu.SemaphoreType.DMA((n,)),
             pltpu.SemaphoreType.DMA,
@@ -277,7 +318,7 @@
 
 
 def build_kernel(
-    ent, yh, yl, th, tl, gram, start, out, weights, order, meta, held, v, sem, meta_sem
+    ent, yh, yl, th, tl, gram, start, out, weights, order, meta, found, place, held, v, sem, meta_sem
 ):
     fetched = pltpu.make_async_copy(
         ent.at[:, pl.ds(3 * TILES, 8), pl.ds(0, 128)], meta, meta_sem
@@ -298,12 +339,38 @@
 
     def scan(c, n):
         for t in range(TILES):
-            order[n] = (c * TILES + t) * (64 * UB) + meta[c, 1, t]
+            found[n] = (c * TILES + t) * (64 * UB) + meta[c, 1, t]
             n = n + jnp.where(meta[c, 0, t] == me, 1, 0)
         return n
 
     n = lax.fori_loop(0, COLS, scan, 0)
     order[LIST - 1] = n
+
+    for b in range(UB):
+        place[b] = 0
+
+    def count(j, _):
+        b = found[j] & (UB - 1)
+        place[b] = place[b] + 1
+        return 0
+
+    lax.fori_loop(0, n, count, 0)
+    total = 0
+    for b in range(UB):
+        of_b = place[b]
+        order[LAST + b] = jnp.where(of_b > 0, total + of_b - 1, -1)
+        place[b] = total
+        total = total + of_b
+
+    def put(j, _):
+        code = found[j]
+        b = code & (UB - 1)
+        to = place[b]
+        order[to] = code
+        place[b] = to + 1
+        return 0
+
+    lax.fori_loop(0, n, put, 0)
     ids = lax.broadcasted_iota(jnp.int32, (BLOCK, NNZ), 0).astype(F32).astype(BF16)
     one, none = jnp.ones((), BF16), jnp.zeros((), BF16)
 
@@ -369,6 +436,8 @@
         out_specs=(VMEM, ANY, SMEM),
         scratch_shapes=[
             pltpu.SMEM((COLS, 8, 128), jnp.int32),
+            pltpu.SMEM((LIST,), jnp.int32),
+            pltpu.SMEM((UB,), jnp.int32),
             pltpu.VMEM((SLOTS, BLOCK, BLOCK), F32),
             pltpu.VMEM((UB * BLOCK, 2 * K), BF16),
             pltpu.SemaphoreType.DMA((SLOTS,)),
@@ -647,29 +716,222 @@
     )(mine)
 
 
-def shards(user_factors, item_factors, fetch_list, tile_user, tile_slot, er, ec, en, tile_count):
-    yh, yl, th, tl, gram, ent = gather(
-        item_factors.reshape(IB, BLOCK, K),
-        fetch_list.reshape(1, 128),
-        tile_user.reshape(1, TILES),
-        tile_slot.reshape(1, TILES),
-        er.reshape(TILES, NNZ),
-        ec.reshape(TILES, NNZ),
-        en.reshape(TILES, NNZ),
-        tile_count.reshape(1, 1),
-    )
-    part, weights, order = build(
-        ent.reshape(COLS, STAGE, NNZ), yh, yl, th, tl, gram, user_factors
-    )
+def cg_kernel(
+    order, part, start, yh, yl, th, tl, gram, weights, out,
+    held, v, x_now, r_now, p_now, pulls, squares, parts, tot, land, sums, near,
+    row_sums, land_x, land_z, half, send_sem, recv_sem, w_sem,
+):
+    _, z, x, along_x, along_z = col_place()
+    load = pltpu.make_async_copy(weights.at[pl.ds(0, FAST)], held, w_sem)
+    load.start()
+    greet(along_x + along_z)
+    copies = Copies(send_sem, recv_sem)
+    send = copies.send
+    far, close, back, end = {}, {}, {}, {}
+    rounds = (part, parts.at[0], parts.at[1])
+
+    def streams(s):
+        for i in (2 * s, 2 * s + 1):
+            way = i % 2 == 0
+            first, second, me = (along_x, along_z, z) if way else (along_z, along_x, x)
+            yield i, pl.ds(SUB * i, SUB), way, first, second, me
+
+    def line(ref, way, d, rows):
+        return ref.at[:, (x + d) % NX, rows] if way else ref.at[(z + d) % NZ, :, rows]
+
+    def begin(k, s):
+        for i, rows, way, first, _, _ in streams(s):
+            far[k, i] = [
+                send(line(rounds[k], way, d, rows), land.at[k, i, d - 1], first[d - 1])
+                for d in (1, 2, 3)
+            ]
+
+    def sum_first(k, s):
+        for i, rows, way, _, second, me in streams(s):
+            for copy in far[k, i]:
+                copy.wait_recv()
+            mine = rounds[k][:, x, rows] if way else rounds[k][z, :, rows]
+            sums[k, i] = mine + land[k, i, 0] + (land[k, i, 1] + land[k, i, 2])
+            close[k, i] = [
+                send(sums.at[k, i, (me + d) % 4], near.at[k, i, d - 1], second[d - 1])
+                for d in (1, 2, 3)
+            ]
+
+    def sum_second(k, s):
+        for i, rows, _, _, second, me in streams(s):
+            for copy in close[k, i]:
+                copy.wait_recv()
+            tot[k, z, x, rows] = sums[k, i, me] + near[k, i, 0] + (near[k, i, 1] + near[k, i, 2])
+            here = tot.at[k, z, x, rows]
+            back[k, i] = [send(here, here, peer) for peer in second]
+
+    def spread(k, s):
+        for i, rows, way, first, _, _ in streams(s):
+            for copy in back[k, i]:
+                copy.wait_recv()
+            here = line(tot.at[k], way, 0, rows)
+            end[k, i] = [send(here, here, peer) for peer in first]
+
+    def arrive(k, s):
+        for i in (2 * s, 2 * s + 1):
+            for copy in end[k, i]:
+                copy.wait_recv()
+
+    g = by_cols(*split(gram[...]))
+    n = order[LIST - 1]
+
+    def compute(k, s, between):
+        rows = pl.ds(64 * s, 64)
+        between[0]()
+
+        def step(b, _):
+            total = tot[k - 1, b // NX, b % NX, rows]
+            if k == 1:
+                p = total - RIDGE * start[b, rows]
+                r_now[b, rows] = p
+            else:
+                before = start[b, rows] if k == 2 else x_now[b, rows]
+                r = r_now[b, rows]
+                old = r if k == 2 else p_now[b, rows]
+                x_now[b, rows], r_now[b, rows], p = update(total, before, r, old)
+            p_now[b, rows] = p
+            v[b, rows] = pair(p)
+            return 0
+
+        lax.fori_loop(0, UB, step, 0, unroll=4)
+
+        def quarter(i, acc):
+            def some(q, acc):
+                last_b, acc = acc
+                for u in range(STEP):
+                    j = i * QUARTER + q * STEP + u
+                    code = order[j]
+                    b, block = code & (UB - 1), (code >> 4) & 63
+                    w = jnp.where(j < n, held[j, rows], 0.0)
+                    scores = fold(dot(v[b, rows], by_cols(th[block], tl[block]), NN))
+                    if k < 3:
+                        pull = fold(dot(pair(w * scores), by_cols(yh[block], yl[block]), NN))
+                    else:
+                        pull = w * scores * scores
+                    acc = jnp.where(b == last_b, acc, 0.0) + pull
+                    last_b = b
+                    pulls[s, j] = acc
+                return last_b, acc
+
+            return lax.fori_loop(0, QUARTER // STEP, some, acc)
+
+        acc = jnp.int32(-1), jnp.zeros((64, K), F32)
+        acc = quarter(0, acc)
+        between[1]()
+        acc = quarter(1, acc)
+        acc = quarter(2, acc)
+        between[2]()
+        acc = quarter(3, acc)
+
+        def close_up(b, _):
+            end_of = order[LAST + b]
+            pulled = jnp.where(end_of >= 0, pulls[s, jnp.maximum(end_of, 0)], 0.0)
+            whole = fold(dot(v[b, rows], g, NN))
+            if k < 3:
+                parts[k - 1, b // NX, b % NX, rows] = whole + pulled
+            else:
+                squares[b, rows] = p_now[b, rows] * whole + pulled
+            return 0
+
+        lax.fori_loop(0, UB, close_up, 0, unroll=4)
+
+    def nothing():
+        pass
+
+    def handlers(k, s):
+        return [functools.partial(f, k, s) for f in (sum_first, sum_second, spread)]
+
+    begin(0, 0)
+    begin(0, 1)
+    for work in (sum_first, sum_second, spread):
+        work(0, 0)
+        work(0, 1)
+    load.wait()
+    arrive(0, 0)
+    compute(1, 0, [nothing] * 3)
+    begin(1, 0)
+    arrive(0, 1)
+    compute(1, 1, handlers(1, 0))
+    begin(1, 1)
+    arrive(1, 0)
+    compute(2, 0, handlers(1, 1))
+    begin(2, 0)
+    arrive(1, 1)
+    compute(2, 1, handlers(2, 0))
+    begin(2, 1)
+    arrive(2, 0)
+    compute(3, 0, handlers(2, 1))
+    arrive(2, 1)
+    compute(3, 1, [nothing] * 3)
+
+    for b in range(UB):
+        row_sums[b : b + 1] = jnp.sum(squares[b].T, axis=0, keepdims=True)
+    for copy in [send(row_sums, land_x.at[i], peer) for i, peer in enumerate(along_x)]:
+        copy.wait_recv()
+    half[...] = row_sums[...] + land_x[0] + (land_x[1] + land_x[2])
+    for copy in [send(half, land_z.at[i], peer) for i, peer in enumerate(along_z)]:
+        copy.wait_recv()
+    both = half[...] + land_z[0] + (land_z[1] + land_z[2])
+    for b in range(UB):
+        p, r = p_now[b], r_now[b]
+        below = jnp.broadcast_to(both[b : b + 1], (BLOCK, BLOCK)).T + RIDGE * dots(p, p)
+        out[b] = x_now[b] + dots(r, r) / (below + EPSILON) * p
+    copies.finish()
+
+
+def all_steps(order, part, start, yh, yl, th, tl, gram, weights):
+    n = BLOCK // SUB
+    copies = 3 * 12 * n + 6
+    blocks = (UB, BLOCK, K)
+    out = pl.pallas_call(
+        cg_kernel,
+        out_shape=jax.ShapeDtypeStruct(blocks, F32),
+        in_specs=[SMEM] + [VMEM] * 7 + [ANY],
+        out_specs=VMEM,
+        scratch_shapes=[
+            pltpu.VMEM((FAST, BLOCK, BLOCK), F32),
+            pltpu.VMEM((UB, BLOCK, 2 * K), BF16),
+            pltpu.VMEM(blocks, F32),
+            pltpu.VMEM(blocks, F32),
+            pltpu.VMEM(blocks, F32),
+            pltpu.VMEM((2, FAST, 64, K), F32),
+            pltpu.VMEM(blocks, F32),
+            pltpu.VMEM((2, NZ, NX, BLOCK, K), F32),
+            pltpu.VMEM((3, NZ, NX, BLOCK, K), F32),
+            pltpu.VMEM((3, n, 3, 4, SUB, K), F32),
+            pltpu.VMEM((3, n, 4, SUB, K), F32),
+            pltpu.VMEM((3, n, 3, SUB, K), F32),
+            pltpu.VMEM((UB, BLOCK), F32),
+            pltpu.VMEM((3, UB, BLOCK), F32),
+            pltpu.VMEM((3, UB, BLOCK), F32),
+            pltpu.VMEM((UB, BLOCK), F32),
+            pltpu.SemaphoreType.DMA((copies,)),
+            pltpu.SemaphoreType.DMA((copies,)),
+            pltpu.SemaphoreType.DMA,
+        ],
+        compiler_params=pltpu.CompilerParams(
+            collective_id=3, has_side_effects=True, vmem_limit_bytes=WHOLE
+        ),
+        name="steps",
+    )(order, part.reshape(NZ, NX, BLOCK, K), start.reshape(blocks), yh, yl, th, tl, gram, weights)
+    return out.reshape(UB * BLOCK, K)
+
+
+def step_by_step(order, part, start, yh, yl, th, tl, gram, weights):
     total = reduce(part)
     tail = [VMEM] * 5 + [ANY]
     part, residual = local(first_kernel, "first", (USERS,) * 2, [SMEM, VMEM, VMEM] + tail)(
-        order, total, user_factors, yh, yl, th, tl, gram, weights
+        order, total, start, yh, yl, th, tl, gram, weights
     )
     total = reduce(part)
     part, iterate, residual, direction = local(
         second_kernel, "second", (USERS,) * 4, [SMEM] + [VMEM] * 3 + tail
-    )(order, total, user_factors, residual, yh, yl, th, tl, gram, weights)
+    )(order, total, start, residual, yh, yl, th, tl, gram, weights)
     total = reduce(part)
     squares = jax.ShapeDtypeStruct((UB, BLOCK), F32)
     part, iterate, residual, direction = local(
@@ -690,6 +952,28 @@
     )(squares, iterate, residual, direction)
 
 
+def shards(user_factors, item_factors, fetch_list, tile_user, tile_slot, er, ec, en, tile_count):
+    yh, yl, th, tl, gram, ent, peak = gather(
+        item_factors.reshape(IB, BLOCK, K),
+        fetch_list.reshape(1, 128),
+        tile_user.reshape(1, TILES),
+        tile_slot.reshape(1, TILES),
+        er.reshape(TILES, NNZ),
+        ec.reshape(TILES, NNZ),
+        en.reshape(TILES, NNZ),
+        tile_count.reshape(1, 1),
+    )
+    part, weights, order = build(
+        ent.reshape(COLS, STAGE, NNZ), yh, yl, th, tl, gram, user_factors
+    )
+    return lax.cond(
+        peak[0, 0] <= FAST,
+        all_steps,
+        step_by_step,
+        order, part, user_factors, yh, yl, th, tl, gram, weights,
+    )
+
+
 def solution(mesh):
     return jax.shard_map(
         shards,

time: 139 us -> 159 us (1.14); the launches traced: 137 us -> 159 us
  Pallas kernels: 136 us -> 156 us
    pallas_call x1, Pallas kernels: 29.3 us -> 40.3 us  [gather(): pl.pallas_call(gather_kernel, out_shape=(*[jax.ShapeDtypeStruct((ROWS * I...]
    pallas_call x8 -> x1, Pallas kernels: 96.6 us -> 104 us  [all_steps(): pl.pallas_call(cg_kernel, out_shape=jax.ShapeDtypeStruct(blocks, F32), in...]
    pallas_call x1, Pallas kernels: 9.59 us -> 11.2 us  [build(): pl.pallas_call(build_kernel, out_shape=(jax.ShapeDtypeStruct((UB * BLOCK,...]
where the time goes in v4:
time: 159 us
  Pallas kernels  156 us (98%)
    pallas_call x1, Pallas kernels, all_steps(): pl.pallas_call(cg_kernel, out_shape=jax.ShapeDtypeStruct(blocks, F32), in...  104 us
    pallas_call x1, Pallas kernels, gather(): pl.pallas_call(gather_kernel, out_shape=(*[jax.ShapeDtypeStruct((ROWS * I...  40.3 us
    pallas_call x1, Pallas kernels, build(): pl.pallas_call(build_kernel, out_shape=(jax.ShapeDtypeStruct((UB * BLOCK,...  11.2 us

profile of v4, /device:TPU:0, one launch (start us, length us, event | category | flops | bytes accessed | tf_op | source)
XLA Modules:
  0.0 159.1 jit_solution(11698849795787414749)
XLA Ops:
  0.7 40.3 %gather.1 = (bf16[64,128,128]{2,1,0:T(8,128)(2,1)S(1)}, bf16[64,128,128]{2,1,0:T(8,128)(2,1)S(1)}, bf16[64,128,128]{2,1,0:T(8,128)(2,1)S(1)}, bf16[64,128,128]{2...) custom-call(f32[8,128,128]{2,1,0:T(8,128)} %bitcast.28, ...), custom_call_target="tpu_custom_call" | custom-call | tf_op jit(solution)/shard_map/gather/pallas_call | solution.py:288
  41.0 0.5 slice.3
  42.2 0.0 copy-start
  42.2 11.2 %build.1 = (f32[2048,128]{1,0:T(8,128)S(1)}, f32[512,128,128]{2,1,0:T(8,128)}, s32[1024]{0:T(1024)S(1)}) custom-call(s32[16,104,512]{2,1,0:T(8,128)S(1)} %bitcast.21, bf16[64,128,128]{2,1,0:T(8,128)(2,1)S(1)} %get-tuple-element.84.yh, bf16[64,128,128]{2,1,0:T(8,128)(2,1)S(1)} %get-tuple-element.85.yl, bf16[64,128,128]{2,1,0:T(8,128)(2,1)S(1)} %get-tuple-element.86.th, ...), custom_call_target="tpu_custom_call" | custom-call | tf_op jit(solution)/shard_map/build/pallas_call | solution.py:428
  53.4 0.0 copy-done
  53.4 104.7 %conditional.1 = (f32[2048,128]{1,0:T(8,128)S(1)}) conditional(s32[]{:T(128)} %bitcast.16, (f32[2048,128]{1,0:T(8,128)S(1)}, s32[1024]{0:T(1024)S(1)}, f32[2048,128]{1,0:T(8,128)S(1)}, bf16[64,128,128]{2,1,0:T(8,128)(2,1)S(1)}, bf16[64,128,128]{2,1,0:T(8,128)(2,1)S(1)}, /*index=5*/bf16[64,128,128]{2,1,0:T(8,128)(2,1)S(1)}, ...), branch_computations={%region_0.0_spmd, %region_1.0_spmd} | conditional | bytes 8 | solution.py:969
  53.6 104.5 %steps.1 = f32[16,128,128]{2,1,0:T(8,128)S(1)} custom-call(s32[1024]{0:T(1024)S(1)} %get-tuple-element.63.order, f32[4,4,128,128]{3,2,1,0:T(8,128)S(1)} %bitcast.26, f32[16,128,128]{2,1,0:T(8,128)S(1)} %bitcast.24, bf16[64,128,128]{2,1,0:T(8,128)(2,1)S(1)} %get-tuple-element.66.yh, bf16[64,128,128]{2,1,0:T(8,128)(2,1)S(1)} %get-tuple-element.67.yl, ...), custom_call_target="tpu_custom_call" | custom-call | tf_op jit(solution)/shard_map/cond/branch_1_fun/steps/pallas_call | solution.py:891
  158.1 1.0 copy.16
Async XLA Ops:
  42.2 11.2 %copy-start = (f32[2048,128]{1,0:T(8,128)S(1)}, f32[2048,128]{1,0:T(8,128)}, u32[]{:S(2)}) copy-start(f32[2048,128]{1,0:T(8,128)} %start.1) | copy-start | bytes 3145732

commit v5 on v4

--- a/solution.py
+++ b/solution.py
@@ -21,8 +21,7 @@
 LIST = 1024
 LAST = 512
 FAST = 40
-QUARTER = 10
-STEP = 5
+STEP = 20
 SUB = 32
 UNROLL = 4
 BUILD = 4
@@ -133,18 +132,6 @@
     ]
     for load in loads:
         load.start()
-    greet(along_x + along_z + [to_right, to_left, to_other])
-    copies = Copies(send_sem, recv_sem)
-    send = copies.send
-
-    half = [items.at[pl.ds(4 * i, 4)] for i in (0, 1)]
-    there = [land.at[r, pl.ds(4 * i, 4)] for i in (0, 1)]
-    from_left, from_right = [None, None], [None, None]
-    for i in (0, 1):
-        from_left[i] = send(half[i], there[i], to_right)
-        from_right[1 - i] = send(half[1 - i], there[1 - i], to_left)
-    between = [send(items, land.at[r], to_other)]
-
     for load in loads[4:]:
         load.wait()
     small[...] = jnp.zeros_like(small)
@@ -158,6 +145,22 @@
     last = 3 * TILES
     stage[last : last + 1, 0:128] = jnp.where(lanes < count[0, 0], slots & (COLS - 1), -1)
     stage[last + 1 : last + 2, 0:128] = ((slots >> 4) * IB + local_id) * UB + small[1:2]
+    first_key = stage[last : last + 1, 0:128]
+    keys[z, x] = jnp.broadcast_to(first_key, (8, 128))
+    greet(along_x + along_z + [to_right, to_left, to_other])
+    copies = Copies(send_sem, recv_sem)
+    send = copies.send
+    mine = keys.at[z, x]
+    told_keys = [send(mine, mine, peer) for peer in along_x]
+
+    half = [items.at[pl.ds(4 * i, 4)] for i in (0, 1)]
+    there = [land.at[r, pl.ds(4 * i, 4)] for i in (0, 1)]
+    from_left, from_right = [None, None], [None, None]
+    for i in (0, 1):
+        from_left[i] = send(half[i], there[i], to_right)
+        from_right[1 - i] = send(half[1 - i], there[1 - i], to_left)
+    between = [send(items, land.at[r], to_other)]
+
     for load in loads[:3]:
         load.wait()
     own = pltpu.make_async_copy(stage, ent.at[z, x], own_sem)
@@ -210,6 +213,24 @@
 
     loads[3].wait()
     sums = add(r, jnp.zeros((K, 2 * K), F32))
+    for copy in told_keys:
+        copy.wait_recv()
+    mine = keys.at[z]
+    told_keys = [send(mine, mine, peer) for peer in along_z]
+
+    def tell(i):
+        return [
+            send(most.at[i], seen.at[i, n], peer)
+            for n, peer in enumerate((to_right, to_left, to_other))
+        ]
+
+    def learn(i, told):
+        for copy in told:
+            copy.wait_recv()
+        most[i + 1] = jnp.maximum(
+            jnp.maximum(most[i], seen[i, 0]), jnp.maximum(seen[i, 1], seen[i, 2])
+        )
+
     for d in (1, 3, 2):
         for w in (0, 1):
             near[w][d].wait_recv()
@@ -223,6 +244,17 @@
     from_right[1].wait_recv()
     piece = land.at[right, pl.ds(4, 4)]
     round_y.append(send(piece, piece, to_left))
+    for copy in told_keys:
+        copy.wait_recv()
+    owners = keys[:, :, 0, :].reshape(COLS, 128)
+    longest = jnp.zeros((1, 1), jnp.int32)
+    for column in range(COLS):
+        here = jnp.where(owners == column, 1, 0)
+        here = jnp.sum(jnp.sum(here, axis=0, keepdims=True), axis=1, keepdims=True)
+        longest = jnp.maximum(longest, here)
+    most[0] = jnp.broadcast_to(longest, (8, 128))
+
+    told = tell(0)
     between[0].wait_recv()
     sums = add(other, sums)
     for d in (1, 3):
@@ -234,57 +266,31 @@
     between.append(send(land.at[right], land.at[right], to_other))
     for w in (0, 1):
         pass_on(w, 2)
+    learn(0, told)
+    told = tell(1)
     sums = add(left, sums)
     sums = add(right, sums)
-    for copy in far:
-        copy.wait_recv()
-    own.wait()
-    load = pltpu.make_async_copy(ent.at[:, :, pl.ds(last, 8), pl.ds(0, 128)], keys, own_sem)
-    load.start()
-    load.wait()
-
-    owners = keys[:, :, 0, :].reshape(COLS, 128)
-    longest = jnp.zeros((1, 1), jnp.int32)
-    for column in range(COLS):
-        here = jnp.where(owners == column, 1, 0)
-        here = jnp.sum(jnp.sum(here, axis=0, keepdims=True), axis=1, keepdims=True)
-        longest = jnp.maximum(longest, here)
-    most[0] = jnp.broadcast_to(longest, (8, 128))
-
-    def tell(i):
-        return [
-            send(most.at[i], seen.at[i, n], peer)
-            for n, peer in enumerate((to_right, to_left, to_other))
-        ]
-
-    def learn(i, told):
-        for copy in told:
-            copy.wait_recv()
-        most[i + 1] = jnp.maximum(
-            jnp.maximum(most[i], seen[i, 0]), jnp.maximum(seen[i, 1], seen[i, 2])
-        )
-
-    told = tell(0)
+    learn(1, told)
+    told = tell(2)
     for copy in round_y:
         copy.wait_recv()
     between.append(send(land.at[across], land.at[across], to_other))
-    learn(0, told)
-    told = tell(1)
     sums = add(across, sums)
-    learn(1, told)
-    told = tell(2)
     for copy, d in zip(between[1:], (3, 1, 2)):
         copy.wait_recv()
         sums = add(((y + d) % NY) * 2 + 1 - core, sums)
     learn(2, told)
     peak[...] = most[3]
+    for copy in far:
+        copy.wait_recv()
+    own.wait()
     mixed = sums[:, K:]
     gram[...] = sums[:, :K] + (mixed + mixed.T)
     copies.finish()
 
 
 def gather(items, fetch, user, slot, er, ec, en, count):
-    n = 6 + 4 + 2 * (3 + 8 + 8) + 9
+    n = 6 + 4 + 2 * (3 + 8 + 8) + 9 + 6
     return pl.pallas_call(
         gather_kernel,
         out_shape=(
@@ -780,9 +786,8 @@
     g = by_cols(*split(gram[...]))
     n = order[LIST - 1]
 
-    def compute(k, s, between):
+    def compute(k, s, before_end):
         rows = pl.ds(64 * s, 64)
-        between[0]()
 
         def step(b, _):
             total = tot[k - 1, b // NX, b % NX, rows]
@@ -798,35 +803,27 @@
             v[b, rows] = pair(p)
             return 0
 
-        lax.fori_loop(0, UB, step, 0, unroll=4)
-
-        def quarter(i, acc):
-            def some(q, acc):
-                last_b, acc = acc
-                for u in range(STEP):
-                    j = i * QUARTER + q * STEP + u
-                    code = order[j]
-                    b, block = code & (UB - 1), (code >> 4) & 63
-                    w = jnp.where(j < n, held[j, rows], 0.0)
-                    scores = fold(dot(v[b, rows], by_cols(th[block], tl[block]), NN))
-                    if k < 3:
-                        pull = fold(dot(pair(w * scores), by_cols(yh[block], yl[block]), NN))
-                    else:
-                        pull = w * scores * scores
-                    acc = jnp.where(b == last_b, acc, 0.0) + pull
-                    last_b = b
-                    pulls[s, j] = acc
-                return last_b, acc
-
-            return lax.fori_loop(0, QUARTER // STEP, some, acc)
-
-        acc = jnp.int32(-1), jnp.zeros((64, K), F32)
-        acc = quarter(0, acc)
-        between[1]()
-        acc = quarter(1, acc)
-        acc = quarter(2, acc)
-        between[2]()
-        acc = quarter(3, acc)
+        lax.fori_loop(0, UB, step, 0, unroll=16)
+
+        def some(q, acc):
+            last_b, acc = acc
+            for u in range(STEP):
+                j = q * STEP + u
+                code = order[j]
+                b, block = code & (UB - 1), (code >> 4) & 63
+                w = jnp.where(j < n, held[j, rows], 0.0)
+                scores = fold(dot(v[b, rows], by_cols(th[block], tl[block]), NN))
+                if k < 3:
+                    pull = fold(dot(pair(w * scores), by_cols(yh[block], yl[block]), NN))
+                else:
+                    pull = w * scores * scores
+                acc = jnp.where(b == last_b, acc, 0.0) + pull
+                last_b = b
+                pulls[s, j] = acc
+            return last_b, acc
+
+        lax.fori_loop(0, FAST // STEP, some, (jnp.int32(-1), jnp.zeros((64, K), F32)))
+        before_end()
 
         def close_up(b, _):
             end_of = order[LAST + b]
@@ -838,36 +835,29 @@
                 squares[b, rows] = p_now[b, rows] * whole + pulled
             return 0
 
-        lax.fori_loop(0, UB, close_up, 0, unroll=4)
+        lax.fori_loop(0, UB, close_up, 0, unroll=16)
 
     def nothing():
         pass
 
-    def handlers(k, s):
-        return [functools.partial(f, k, s) for f in (sum_first, sum_second, spread)]
-
     begin(0, 0)
     begin(0, 1)
-    for work in (sum_first, sum_second, spread):
-        work(0, 0)
-        work(0, 1)
-    load.wait()
-    arrive(0, 0)
-    compute(1, 0, [nothing] * 3)
-    begin(1, 0)
-    arrive(0, 1)
-    compute(1, 1, handlers(1, 0))
-    begin(1, 1)
-    arrive(1, 0)
-    compute(2, 0, handlers(1, 1))
-    begin(2, 0)
-    arrive(1, 1)
-    compute(2, 1, handlers(2, 0))
-    begin(2, 1)
-    arrive(2, 0)
-    compute(3, 0, handlers(2, 1))
-    arrive(2, 1)
-    compute(3, 1, [nothing] * 3)
+    sum_first(0, 0)
+    for k in range(3):
+        sum_first(k, 1)
+        for work in (sum_second, spread):
+            work(k, 0)
+            work(k, 1)
+        if k == 0:
+            load.wait()
+        arrive(k, 0)
+        compute(k + 1, 0, nothing)
+        if k < 2:
+            begin(k + 1, 0)
+        arrive(k, 1)
+        compute(k + 1, 1, functools.partial(sum_first, k + 1, 0) if k < 2 else nothing)
+        if k < 2:
+            begin(k + 1, 1)
 
     for b in range(UB):
         row_sums[b : b + 1] = jnp.sum(squares[b].T, axis=0, keepdims=True)

time: 159 us -> 139 us (0.87)
  Pallas kernels: 156 us -> 136 us
    pallas_call x1, Pallas kernels: 104 us -> 91.7 us  [all_steps(): pl.pallas_call(cg_kernel, out_shape=jax.ShapeDtypeStruct(blocks, F32), in...]
    pallas_call x1, Pallas kernels: 40.3 us -> 34.5 us  [gather(): pl.pallas_call(gather_kernel, out_shape=(*[jax.ShapeDtypeStruct((ROWS * I...]
where the time goes in v5:
time: 139 us
  Pallas kernels  136 us (98%)
  local copies, waits for them, and re-layouts  1.49 us (1%)
    pallas_call x1, Pallas kernels, all_steps(): pl.pallas_call(cg_kernel, out_shape=jax.ShapeDtypeStruct(blocks, F32), in...  91.7 us
    pallas_call x1, Pallas kernels, gather(): pl.pallas_call(gather_kernel, out_shape=(*[jax.ShapeDtypeStruct((ROWS * I...  34.5 us
    pallas_call x1, Pallas kernels, build(): pl.pallas_call(build_kernel, out_shape=(jax.ShapeDtypeStruct((UB * BLOCK,...  9.93 us

profile of v5, /device:TPU:0, one launch (start us, length us, event | category | flops | bytes accessed | tf_op | source)
XLA Modules:
  0.0 139.2 jit_solution(8745841056661119574)
XLA Ops:
  0.7 34.5 %gather.1 = (bf16[64,128,128]{2,1,0:T(8,128)(2,1)S(1)}, bf16[64,128,128]{2,1,0:T(8,128)(2,1)S(1)}, bf16[64,128,128]{2,1,0:T(8,128)(2,1)S(1)}, bf16[64,128,128]{2...) custom-call(f32[8,128,128]{2,1,0:T(8,128)} %bitcast.28, ...), custom_call_target="tpu_custom_call" | custom-call | tf_op jit(solution)/shard_map/gather/pallas_call | solution.py:294
  35.1 0.5 slice.3
  36.3 0.0 copy-start
  36.3 9.9 %build.1 = (f32[2048,128]{1,0:T(8,128)S(1)}, f32[512,128,128]{2,1,0:T(8,128)}, s32[1024]{0:T(1024)S(1)}) custom-call(s32[16,104,512]{2,1,0:T(8,128)S(1)} %bitcast.21, bf16[64,128,128]{2,1,0:T(8,128)(2,1)S(1)} %get-tuple-element.84.yh, bf16[64,128,128]{2,1,0:T(8,128)(2,1)S(1)} %get-tuple-element.85.yl, bf16[64,128,128]{2,1,0:T(8,128)(2,1)S(1)} %get-tuple-element.86.th, ...), custom_call_target="tpu_custom_call" | custom-call | tf_op jit(solution)/shard_map/build/pallas_call | solution.py:434
  46.3 0.0 copy-done
  46.3 91.9 %conditional.1 = (f32[2048,128]{1,0:T(8,128)S(1)}) conditional(s32[]{:T(128)} %bitcast.16, (f32[2048,128]{1,0:T(8,128)S(1)}, s32[1024]{0:T(1024)S(1)}, f32[2048,128]{1,0:T(8,128)S(1)}, bf16[64,128,128]{2,1,0:T(8,128)(2,1)S(1)}, bf16[64,128,128]{2,1,0:T(8,128)(2,1)S(1)}, /*index=5*/bf16[64,128,128]{2,1,0:T(8,128)(2,1)S(1)}, ...), branch_computations={%region_0.0_spmd, %region_1.0_spmd} | conditional | bytes 8 | solution.py:959
  46.3 91.7 %steps.1 = f32[16,128,128]{2,1,0:T(8,128)S(1)} custom-call(s32[1024]{0:T(1024)S(1)} %get-tuple-element.63.order, f32[4,4,128,128]{3,2,1,0:T(8,128)S(1)} %bitcast.26, f32[16,128,128]{2,1,0:T(8,128)S(1)} %bitcast.24, bf16[64,128,128]{2,1,0:T(8,128)(2,1)S(1)} %get-tuple-element.66.yh, bf16[64,128,128]{2,1,0:T(8,128)(2,1)S(1)} %get-tuple-element.67.yl, ...), custom_call_target="tpu_custom_call" | custom-call | tf_op jit(solution)/shard_map/cond/branch_1_fun/steps/pallas_call | solution.py:881
  138.2 1.0 copy.16
Async XLA Ops:
  36.3 9.9 %copy-start = (f32[2048,128]{1,0:T(8,128)S(1)}, f32[2048,128]{1,0:T(8,128)}, u32[]{:S(2)}) copy-start(f32[2048,128]{1,0:T(8,128)} %start.1) | copy-start | bytes 3145732

commit v6 on v5

--- a/solution.py
+++ b/solution.py
@@ -20,8 +20,8 @@
 ALL_TILES = COLS * TILES
 LIST = 1024
 LAST = 512
-FAST = 40
-STEP = 20
+FAST = 36
+STEP = 18
 SUB = 32
 UNROLL = 4
 BUILD = 4
@@ -116,6 +116,7 @@
     right, left, across = (((y + d) % NY) * 2 + core for d in (1, 3, 2))
     other = y * 2 + 1 - core
     to_right, to_left, to_other = {"row": right}, {"row": left}, {"row": other}
+    to_across = {"row": across}
     loads = [
         pltpu.make_async_copy(src, dst, in_sem.at[i])
         for i, (src, dst) in enumerate(
@@ -132,6 +133,17 @@
     ]
     for load in loads:
         load.start()
+    greet(along_x + along_z + [to_right, to_left, to_across, to_other])
+    copies = Copies(send_sem, recv_sem)
+    send = copies.send
+    half = [items.at[pl.ds(4 * i, 4)] for i in (0, 1)]
+    there = [land.at[r, pl.ds(4 * i, 4)] for i in (0, 1)]
+    from_left, from_right = [None, None], [None, None]
+    for i in (0, 1):
+        from_left[i] = send(half[i], there[i], to_right)
+        from_right[1 - i] = send(half[1 - i], there[1 - i], to_left)
+    between = [send(items, land.at[r], to_other)]
+
     for load in loads[4:]:
         load.wait()
     small[...] = jnp.zeros_like(small)
@@ -147,20 +159,6 @@
     stage[last + 1 : last + 2, 0:128] = ((slots >> 4) * IB + local_id) * UB + small[1:2]
     first_key = stage[last : last + 1, 0:128]
     keys[z, x] = jnp.broadcast_to(first_key, (8, 128))
-    greet(along_x + along_z + [to_right, to_left, to_other])
-    copies = Copies(send_sem, recv_sem)
-    send = copies.send
-    mine = keys.at[z, x]
-    told_keys = [send(mine, mine, peer) for peer in along_x]
-
-    half = [items.at[pl.ds(4 * i, 4)] for i in (0, 1)]
-    there = [land.at[r, pl.ds(4 * i, 4)] for i in (0, 1)]
-    from_left, from_right = [None, None], [None, None]
-    for i in (0, 1):
-        from_left[i] = send(half[i], there[i], to_right)
-        from_right[1 - i] = send(half[1 - i], there[1 - i], to_left)
-    between = [send(items, land.at[r], to_other)]
-
     for load in loads[:3]:
         load.wait()
     own = pltpu.make_async_copy(stage, ent.at[z, x], own_sem)
@@ -186,6 +184,8 @@
         for d in (1, 3, 2):
             near[w][d] = send(stage.at[rows], at(0, 0).at[rows], along[d - 1])
         spread(w, 0, stage.at[rows])
+    mine = keys.at[z, x]
+    told_keys = [send(mine, mine, peer) for peer in along_x]
 
     far = []
 
@@ -217,19 +217,6 @@
         copy.wait_recv()
     mine = keys.at[z]
     told_keys = [send(mine, mine, peer) for peer in along_z]
-
-    def tell(i):
-        return [
-            send(most.at[i], seen.at[i, n], peer)
-            for n, peer in enumerate((to_right, to_left, to_other))
-        ]
-
-    def learn(i, told):
-        for copy in told:
-            copy.wait_recv()
-        most[i + 1] = jnp.maximum(
-            jnp.maximum(most[i], seen[i, 0]), jnp.maximum(seen[i, 1], seen[i, 2])
-        )
 
     for d in (1, 3, 2):
         for w in (0, 1):
@@ -254,7 +241,10 @@
         longest = jnp.maximum(longest, here)
     most[0] = jnp.broadcast_to(longest, (8, 128))
 
-    told = tell(0)
+    told = [
+        send(most.at[0], seen.at[i], peer)
+        for i, peer in enumerate((to_right, to_left, to_across))
+    ]
     between[0].wait_recv()
     sums = add(other, sums)
     for d in (1, 3):
@@ -266,12 +256,12 @@
     between.append(send(land.at[right], land.at[right], to_other))
     for w in (0, 1):
         pass_on(w, 2)
-    learn(0, told)
-    told = tell(1)
+    for copy in told:
+        copy.wait_recv()
+    most[1] = jnp.maximum(jnp.maximum(most[0], seen[0]), jnp.maximum(seen[1], seen[2]))
+    told = send(most.at[1], seen.at[3], to_other)
     sums = add(left, sums)
     sums = add(right, sums)
-    learn(1, told)
-    told = tell(2)
     for copy in round_y:
         copy.wait_recv()
     between.append(send(land.at[across], land.at[across], to_other))
@@ -279,8 +269,8 @@
     for copy, d in zip(between[1:], (3, 1, 2)):
         copy.wait_recv()
         sums = add(((y + d) % NY) * 2 + 1 - core, sums)
-    learn(2, told)
-    peak[...] = most[3]
+    told.wait_recv()
+    peak[...] = jnp.maximum(most[1], seen[3])
     for copy in far:
         copy.wait_recv()
     own.wait()
@@ -290,7 +280,7 @@
 
 
 def gather(items, fetch, user, slot, er, ec, en, count):
-    n = 6 + 4 + 2 * (3 + 8 + 8) + 9 + 6
+    n = 6 + 4 + 2 * (3 + 8 + 8) + 10
     return pl.pallas_call(
         gather_kernel,
         out_shape=(
@@ -309,8 +299,8 @@
             pltpu.VMEM((1, TILES), jnp.int32),
             pltpu.VMEM((8, 128), jnp.int32),
             pltpu.VMEM((NZ, NX, 8, 128), jnp.int32),
+            pltpu.VMEM((2, 8, 128), jnp.int32),
             pltpu.VMEM((4, 8, 128), jnp.int32),
-            pltpu.VMEM((3, 3, 8, 128), jnp.int32),
             pltpu.SemaphoreType.DMA((n,)),
             pltpu.SemaphoreType.DMA((n,)),
             pltpu.SemaphoreType.DMA,
@@ -377,7 +367,7 @@
         return 0
 
     lax.fori_loop(0, n, put, 0)
-    ids = lax.broadcasted_iota(jnp.int32, (BLOCK, NNZ), 0).astype(F32).astype(BF16)
+    ids = lax.broadcasted_iota(jnp.int32, (BLOCK, NNZ), 0)
     one, none = jnp.ones((), BF16), jnp.zeros((), BF16)
 
     def out_copy(j):
@@ -392,25 +382,34 @@
             def _(j=j):
                 out_copy(j - SLOTS).wait()
 
+        made = []
         for u in range(BUILD):
             j = q * BUILD + u
             code = jnp.where(j < n, order[j], 0)
             b, block, at = code % UB, (code // UB) % 64, code // (64 * UB)
             c, t = at // TILES, at % TILES
-            rows = jnp.where(j < n, ent[c, pl.ds(t, 1), :], BLOCK).astype(F32).astype(BF16)
-            cols = ent[c, pl.ds(TILES + t, 1), :].astype(F32).astype(BF16)
-            counts = ent[c, pl.ds(2 * TILES + t, 1), :].astype(F32).astype(BF16)
-            row_hot = ids == rows
-            col_hot = jnp.where(ids == cols, one, none)
-            ones = jnp.where(row_hot, one, none)
-            many = jnp.where(row_hot, counts, none)
-            both = dot(jnp.concatenate([ones, many], axis=0), col_hot, NT)
-            excess = SCALE * both[BLOCK:]
-            held[j % SLOTS] = excess
-            where = rows_of(b)
-            scores = fold(dot(v[where], by_cols(th[block], tl[block]), NN))
-            pull = both[:BLOCK] + excess * (1.0 - scores)
-            out[where] += fold(dot(pair(pull), by_cols(yh[block], yl[block]), NN))
+            rows = jnp.where(j < n, ent[c, pl.ds(t, 1), :], BLOCK)
+            cols = ent[c, pl.ds(TILES + t, 1), :]
+            counts = ent[c, pl.ds(2 * TILES + t, 1), :].astype(F32)
+            in_col = ids == cols
+            once = jnp.where(in_col, 1.0, 0.0).astype(BF16)
+            ones = jnp.where(ids == rows, 1.0, 0.0).astype(BF16)
+            many = jnp.where(in_col, counts, 0.0).astype(BF16)
+            both = dot(ones, jnp.concatenate([once, many], axis=0), NT)
+            times, excess = both[:, :BLOCK], SCALE * both[:, BLOCK:]
+            made.append((rows_of(b), block, times, excess))
+        scores = [
+            fold(dot(v[where], by_cols(th[block], tl[block]), NN)) for where, block, _, _ in made
+        ]
+        pulls = [
+            fold(
+                dot(pair(times + excess * (1.0 - score)), by_cols(yh[block], yl[block]), NN)
+            )
+            for (_, block, times, excess), score in zip(made, scores)
+        ]
+        for u, ((where, _, _, excess), pull) in enumerate(zip(made, pulls)):
+            held[(q * BUILD + u) % SLOTS] = excess
+            out[where] += pull
         for u in range(BUILD):
             j = q * BUILD + u
 

time: 139 us -> 133 us (0.957)
  Pallas kernels: 136 us -> 129 us
    pallas_call x1, Pallas kernels: 91.7 us -> 87 us  [all_steps(): pl.pallas_call(cg_kernel, out_shape=jax.ShapeDtypeStruct(blocks, F32), in...]
where the time goes in v6:
time: 133 us; the launch traced here: 132 us
  Pallas kernels  129 us (97%)
  local copies, waits for them, and re-layouts  1.49 us (1%)
  between operations  1.35 us (1%)
    pallas_call x1, Pallas kernels, all_steps(): pl.pallas_call(cg_kernel, out_shape=jax.ShapeDtypeStruct(blocks, F32), in...  87 us
    pallas_call x1, Pallas kernels, gather(): pl.pallas_call(gather_kernel, out_shape=(*[jax.ShapeDtypeStruct((ROWS * I...  33.4 us
    pallas_call x1, Pallas kernels, build(): pl.pallas_call(build_kernel, out_shape=(jax.ShapeDtypeStruct((UB * BLOCK,...  9.03 us

profile of v6, /device:TPU:0, one launch (start us, length us, event | category | flops | bytes accessed | tf_op | source)
XLA Modules:
  0.0 132.4 jit_solution(13924181725023897154)
XLA Ops:
  0.7 33.4 %gather.1 = (bf16[64,128,128]{2,1,0:T(8,128)(2,1)S(1)}, bf16[64,128,128]{2,1,0:T(8,128)(2,1)S(1)}, bf16[64,128,128]{2,1,0:T(8,128)(2,1)S(1)}, bf16[64,128,128]{2...) custom-call(f32[8,128,128]{2,1,0:T(8,128)} %bitcast.28, ...), custom_call_target="tpu_custom_call" | custom-call | tf_op jit(solution)/shard_map/gather/pallas_call | solution.py:284
  34.0 0.5 slice.3
  35.2 0.0 copy-start
  35.2 9.0 %build.1 = (f32[2048,128]{1,0:T(8,128)S(1)}, f32[512,128,128]{2,1,0:T(8,128)}, s32[1024]{0:T(1024)S(1)}) custom-call(s32[16,104,512]{2,1,0:T(8,128)S(1)} %bitcast.21, bf16[64,128,128]{2,1,0:T(8,128)(2,1)S(1)} %get-tuple-element.84.yh, bf16[64,128,128]{2,1,0:T(8,128)(2,1)S(1)} %get-tuple-element.85.yl, bf16[64,128,128]{2,1,0:T(8,128)(2,1)S(1)} %get-tuple-element.86.th, ...), custom_call_target="tpu_custom_call" | custom-call | tf_op jit(solution)/shard_map/build/pallas_call | solution.py:433
  44.2 0.0 copy-done
  44.2 87.2 %conditional.1 = (f32[2048,128]{1,0:T(8,128)S(1)}) conditional(s32[]{:T(128)} %bitcast.16, (f32[2048,128]{1,0:T(8,128)S(1)}, s32[1024]{0:T(1024)S(1)}, f32[2048,128]{1,0:T(8,128)S(1)}, bf16[64,128,128]{2,1,0:T(8,128)(2,1)S(1)}, bf16[64,128,128]{2,1,0:T(8,128)(2,1)S(1)}, /*index=5*/bf16[64,128,128]{2,1,0:T(8,128)(2,1)S(1)}, ...), branch_computations={%region_0.0_spmd, %region_1.0_spmd} | conditional | bytes 8 | solution.py:958
  44.4 87.0 %steps.1 = f32[16,128,128]{2,1,0:T(8,128)S(1)} custom-call(s32[1024]{0:T(1024)S(1)} %get-tuple-element.63.order, f32[4,4,128,128]{3,2,1,0:T(8,128)S(1)} %bitcast.26, f32[16,128,128]{2,1,0:T(8,128)S(1)} %bitcast.24, bf16[64,128,128]{2,1,0:T(8,128)(2,1)S(1)} %get-tuple-element.66.yh, bf16[64,128,128]{2,1,0:T(8,128)(2,1)S(1)} %get-tuple-element.67.yl, ...), custom_call_target="tpu_custom_call" | custom-call | tf_op jit(solution)/shard_map/cond/branch_1_fun/steps/pallas_call | solution.py:880
  131.4 1.0 copy.16
Async XLA Ops:
  35.2 9.1 %copy-start = (f32[2048,128]{1,0:T(8,128)S(1)}, f32[2048,128]{1,0:T(8,128)}, u32[]{:S(2)}) copy-start(f32[2048,128]{1,0:T(8,128)} %start.1) | copy-start | bytes 3145732

commit v7 on v6

--- a/solution.py
+++ b/solution.py
@@ -234,11 +234,12 @@
     for copy in told_keys:
         copy.wait_recv()
     owners = keys[:, :, 0, :].reshape(COLS, 128)
-    longest = jnp.zeros((1, 1), jnp.int32)
-    for column in range(COLS):
-        here = jnp.where(owners == column, 1, 0)
-        here = jnp.sum(jnp.sum(here, axis=0, keepdims=True), axis=1, keepdims=True)
-        longest = jnp.maximum(longest, here)
+    counted = [
+        jnp.sum(jnp.where(owners == column, 1.0, 0.0), axis=0, keepdims=True)
+        for column in range(COLS)
+    ]
+    counted = jnp.sum(jnp.concatenate(counted, axis=0), axis=1, keepdims=True)
+    longest = jnp.max(counted, axis=0, keepdims=True).astype(jnp.int32)
     most[0] = jnp.broadcast_to(longest, (8, 128))
 
     told = [
@@ -748,7 +749,7 @@
         for i, rows, way, first, _, _ in streams(s):
             far[k, i] = [
                 send(line(rounds[k], way, d, rows), land.at[k, i, d - 1], first[d - 1])
-                for d in (1, 2, 3)
+                for d in (2, 1, 3)
             ]
 
     def sum_first(k, s):
@@ -759,7 +760,7 @@
             sums[k, i] = mine + land[k, i, 0] + (land[k, i, 1] + land[k, i, 2])
             close[k, i] = [
                 send(sums.at[k, i, (me + d) % 4], near.at[k, i, d - 1], second[d - 1])
-                for d in (1, 2, 3)
+                for d in (2, 1, 3)
             ]
 
     def sum_second(k, s):
@@ -768,14 +769,14 @@
                 copy.wait_recv()
             tot[k, z, x, rows] = sums[k, i, me] + near[k, i, 0] + (near[k, i, 1] + near[k, i, 2])
             here = tot.at[k, z, x, rows]
-            back[k, i] = [send(here, here, peer) for peer in second]
+            back[k, i] = [send(here, here, second[d]) for d in (1, 0, 2)]
 
     def spread(k, s):
         for i, rows, way, first, _, _ in streams(s):
             for copy in back[k, i]:
                 copy.wait_recv()
             here = line(tot.at[k], way, 0, rows)
-            end[k, i] = [send(here, here, peer) for peer in first]
+            end[k, i] = [send(here, here, first[d]) for d in (1, 0, 2)]
 
     def arrive(k, s):
         for i in (2 * s, 2 * s + 1):
@@ -835,6 +836,11 @@
             return 0
 
         lax.fori_loop(0, UB, close_up, 0, unroll=16)
+        if k == 3:
+            for b in range(UB):
+                row_sums[b : b + 1, 64 * s : 64 * s + 64] = jnp.sum(
+                    squares[b, rows].T, axis=0, keepdims=True
+                )
 
     def nothing():
         pass
@@ -858,18 +864,23 @@
         if k < 2:
             begin(k + 1, 1)
 
+    told = [send(row_sums, land_x.at[i], peer) for i, peer in enumerate(along_x)]
     for b in range(UB):
-        row_sums[b : b + 1] = jnp.sum(squares[b].T, axis=0, keepdims=True)
-    for copy in [send(row_sums, land_x.at[i], peer) for i, peer in enumerate(along_x)]:
+        p, r = p_now[b], r_now[b]
+        rest = jnp.broadcast_to(RIDGE * dots(p, p) + EPSILON, (BLOCK, K))
+        pulls[0, b] = rest[:64]
+        pulls[1, b] = rest[64:]
+        squares[b] = jnp.broadcast_to(dots(r, r), (BLOCK, K))
+    for copy in told:
         copy.wait_recv()
     half[...] = row_sums[...] + land_x[0] + (land_x[1] + land_x[2])
     for copy in [send(half, land_z.at[i], peer) for i, peer in enumerate(along_z)]:
         copy.wait_recv()
     both = half[...] + land_z[0] + (land_z[1] + land_z[2])
     for b in range(UB):
-        p, r = p_now[b], r_now[b]
-        below = jnp.broadcast_to(both[b : b + 1], (BLOCK, BLOCK)).T + RIDGE * dots(p, p)
-        out[b] = x_now[b] + dots(r, r) / (below + EPSILON) * p
+        below = jnp.broadcast_to(both[b : b + 1], (BLOCK, BLOCK)).T
+        rest = jnp.concatenate([pulls[0, b], pulls[1, b]], axis=0)
+        out[b] = x_now[b] + squares[b] / (below + rest) * p_now[b]
     copies.finish()
 
 

time: 133 us -> 133 us (level)
    pallas_call x1, Pallas kernels: 9.03 us -> 13 us  [build(): pl.pallas_call(build_kernel, out_shape=(jax.ShapeDtypeStruct((UB * BLOCK,...]
    pallas_call x1, Pallas kernels: 87 us -> 83.2 us  [all_steps(): pl.pallas_call(cg_kernel, out_shape=jax.ShapeDtypeStruct(blocks, F32), in...]
where the time goes in v7:
time: 133 us
  Pallas kernels  130 us (98%)
  local copies, waits for them, and re-layouts  1.49 us (1%)
  between operations  1.35 us (1%)
    pallas_call x1, Pallas kernels, all_steps(): pl.pallas_call(cg_kernel, out_shape=jax.ShapeDtypeStruct(blocks, F32), in...  83.2 us
    pallas_call x1, Pallas kernels, gather(): pl.pallas_call(gather_kernel, out_shape=(*[jax.ShapeDtypeStruct((ROWS * I...  33.4 us
    pallas_call x1, Pallas kernels, build(): pl.pallas_call(build_kernel, out_shape=(jax.ShapeDtypeStruct((UB * BLOCK,...  13 us

profile of v7, /device:TPU:0, one launch (start us, length us, event | category | flops | bytes accessed | tf_op | source)
XLA Modules:
  0.0 132.6 jit_solution(15031176658558272095)
XLA Ops:
  0.7 33.4 %gather.1 = (bf16[64,128,128]{2,1,0:T(8,128)(2,1)S(1)}, bf16[64,128,128]{2,1,0:T(8,128)(2,1)S(1)}, bf16[64,128,128]{2,1,0:T(8,128)(2,1)S(1)}, bf16[64,128,128]{2...) custom-call(f32[8,128,128]{2,1,0:T(8,128)} %bitcast.28, ...), custom_call_target="tpu_custom_call" | custom-call | tf_op jit(solution)/shard_map/gather/pallas_call | solution.py:285
  34.0 0.5 slice.3
  35.2 0.0 copy-start
  35.2 13.0 %build.1 = (f32[2048,128]{1,0:T(8,128)S(1)}, f32[512,128,128]{2,1,0:T(8,128)}, s32[1024]{0:T(1024)S(1)}) custom-call(s32[16,104,512]{2,1,0:T(8,128)S(1)} %bitcast.21, bf16[64,128,128]{2,1,0:T(8,128)(2,1)S(1)} %get-tuple-element.84.yh, bf16[64,128,128]{2,1,0:T(8,128)(2,1)S(1)} %get-tuple-element.85.yl, bf16[64,128,128]{2,1,0:T(8,128)(2,1)S(1)} %get-tuple-element.86.th, ...), custom_call_target="tpu_custom_call" | custom-call | tf_op jit(solution)/shard_map/build/pallas_call | solution.py:434
  48.2 0.0 copy-done
  48.2 83.4 %conditional.1 = (f32[2048,128]{1,0:T(8,128)S(1)}) conditional(s32[]{:T(128)} %bitcast.16, (f32[2048,128]{1,0:T(8,128)S(1)}, s32[1024]{0:T(1024)S(1)}, f32[2048,128]{1,0:T(8,128)S(1)}, bf16[64,128,128]{2,1,0:T(8,128)(2,1)S(1)}, bf16[64,128,128]{2,1,0:T(8,128)(2,1)S(1)}, /*index=5*/bf16[64,128,128]{2,1,0:T(8,128)(2,1)S(1)}, ...), branch_computations={%region_0.0_spmd, %region_1.0_spmd} | conditional | bytes 8 | solution.py:969
  48.2 83.2 %steps.1 = f32[16,128,128]{2,1,0:T(8,128)S(1)} custom-call(s32[1024]{0:T(1024)S(1)} %get-tuple-element.63.order, f32[4,4,128,128]{3,2,1,0:T(8,128)S(1)} %bitcast.26, f32[16,128,128]{2,1,0:T(8,128)S(1)} %bitcast.24, bf16[64,128,128]{2,1,0:T(8,128)(2,1)S(1)} %get-tuple-element.66.yh, bf16[64,128,128]{2,1,0:T(8,128)(2,1)S(1)} %get-tuple-element.67.yl, ...), custom_call_target="tpu_custom_call" | custom-call | tf_op jit(solution)/shard_map/cond/branch_1_fun/steps/pallas_call | solution.py:891
  131.6 1.0 copy.16
Async XLA Ops:
  35.2 13.0 %copy-start = (f32[2048,128]{1,0:T(8,128)S(1)}, f32[2048,128]{1,0:T(8,128)}, u32[]{:S(2)}) copy-start(f32[2048,128]{1,0:T(8,128)} %start.1) | copy-start | bytes 3145732

commit v8 on v7

--- a/solution.py
+++ b/solution.py
@@ -23,6 +23,7 @@
 FAST = 36
 STEP = 18
 SUB = 32
+THIN = 16
 UNROLL = 4
 BUILD = 4
 SLOTS = 2 * BUILD
@@ -315,7 +316,7 @@
 
 
 def build_kernel(
-    ent, yh, yl, th, tl, gram, start, out, weights, order, meta, found, place, held, v, sem, meta_sem
+    ent, yh, yl, th, tl, gram, start, peak, out, weights, order, fits, meta, found, place, held, v, sem, meta_sem
 ):
     fetched = pltpu.make_async_copy(
         ent.at[:, pl.ds(3 * TILES, 8), pl.ds(0, 128)], meta, meta_sem
@@ -331,6 +332,7 @@
         return 0
 
     lax.fori_loop(0, UB, begin, 0, unroll=UNROLL)
+    fits[0] = jnp.where(jnp.max(peak[...].astype(F32)) <= FAST, 1, 0)
     fetched.wait()
     me = lax.axis_index("col")
 
@@ -430,16 +432,17 @@
     lax.fori_loop(jnp.maximum(groups * BUILD - SLOTS, 0), n, drain, 0)
 
 
-def build(ent, yh, yl, th, tl, gram, start):
+def build(ent, yh, yl, th, tl, gram, start, peak):
     return pl.pallas_call(
         build_kernel,
         out_shape=(
             jax.ShapeDtypeStruct((UB * BLOCK, K), F32),
             jax.ShapeDtypeStruct((ALL_TILES, BLOCK, BLOCK), F32),
             jax.ShapeDtypeStruct((LIST,), jnp.int32),
+            jax.ShapeDtypeStruct((1,), jnp.int32),
         ),
-        in_specs=[VMEM] * 7,
-        out_specs=(VMEM, ANY, SMEM),
+        in_specs=[VMEM] * 8,
+        out_specs=(VMEM, ANY, SMEM, SMEM),
         scratch_shapes=[
             pltpu.SMEM((COLS, 8, 128), jnp.int32),
             pltpu.SMEM((LIST,), jnp.int32),
@@ -451,7 +454,7 @@
         ],
         compiler_params=pltpu.CompilerParams(vmem_limit_bytes=BIG),
         name="build",
-    )(ent, yh, yl, th, tl, gram, start)
+    )(ent, yh, yl, th, tl, gram, start, peak)
 
 
 def fetch_tiles(order, weights, held, sem, base):
@@ -737,10 +740,10 @@
     rounds = (part, parts.at[0], parts.at[1])
 
     def streams(s):
-        for i in (2 * s, 2 * s + 1):
+        for i in range(4 * s, 4 * s + 4):
             way = i % 2 == 0
             first, second, me = (along_x, along_z, z) if way else (along_z, along_x, x)
-            yield i, pl.ds(SUB * i, SUB), way, first, second, me
+            yield i, pl.ds(THIN * i, THIN), way, first, second, me
 
     def line(ref, way, d, rows):
         return ref.at[:, (x + d) % NX, rows] if way else ref.at[(z + d) % NZ, :, rows]
@@ -779,7 +782,7 @@
             end[k, i] = [send(here, here, first[d]) for d in (1, 0, 2)]
 
     def arrive(k, s):
-        for i in (2 * s, 2 * s + 1):
+        for i in range(4 * s, 4 * s + 4):
             for copy in end[k, i]:
                 copy.wait_recv()
 
@@ -885,7 +888,7 @@
 
 
 def all_steps(order, part, start, yh, yl, th, tl, gram, weights):
-    n = BLOCK // SUB
+    n = BLOCK // THIN
     copies = 3 * 12 * n + 6
     blocks = (UB, BLOCK, K)
     out = pl.pallas_call(
@@ -903,9 +906,9 @@
             pltpu.VMEM(blocks, F32),
             pltpu.VMEM((2, NZ, NX, BLOCK, K), F32),
             pltpu.VMEM((3, NZ, NX, BLOCK, K), F32),
-            pltpu.VMEM((3, n, 3, 4, SUB, K), F32),
-            pltpu.VMEM((3, n, 4, SUB, K), F32),
-            pltpu.VMEM((3, n, 3, SUB, K), F32),
+            pltpu.VMEM((3, n, 3, 4, THIN, K), F32),
+            pltpu.VMEM((3, n, 4, THIN, K), F32),
+            pltpu.VMEM((3, n, 3, THIN, K), F32),
             pltpu.VMEM((UB, BLOCK), F32),
             pltpu.VMEM((3, UB, BLOCK), F32),
             pltpu.VMEM((3, UB, BLOCK), F32),
@@ -963,11 +966,11 @@
         en.reshape(TILES, NNZ),
         tile_count.reshape(1, 1),
     )
-    part, weights, order = build(
-        ent.reshape(COLS, STAGE, NNZ), yh, yl, th, tl, gram, user_factors
+    part, weights, order, fits = build(
+        ent.reshape(COLS, STAGE, NNZ), yh, yl, th, tl, gram, user_factors, peak
     )
     return lax.cond(
-        peak[0, 0] <= FAST,
+        fits[0] > 0,
         all_steps,
         step_by_step,
         order, part, user_factors, yh, yl, th, tl, gram, weights,

time: 133 us -> 132 us (level)
    pallas_call x1, Pallas kernels: 13 us -> 9.08 us  [build(): pl.pallas_call(build_kernel, out_shape=(jax.ShapeDtypeStruct((UB * BLOCK,...]
    pallas_call x1, Pallas kernels: 83.2 us -> 86.2 us  [all_steps(): pl.pallas_call(cg_kernel, out_shape=jax.ShapeDtypeStruct(blocks, F32), in...]
where the time goes in v8:
time: 132 us; the launch traced here: 131 us
  Pallas kernels  129 us (98%)
  between operations  1.34 us (1%)
    pallas_call x1, Pallas kernels, all_steps(): pl.pallas_call(cg_kernel, out_shape=jax.ShapeDtypeStruct(blocks, F32), in...  86.2 us
    pallas_call x1, Pallas kernels, gather(): pl.pallas_call(gather_kernel, out_shape=(*[jax.ShapeDtypeStruct((ROWS * I...  33.4 us
    pallas_call x1, Pallas kernels, build(): pl.pallas_call(build_kernel, out_shape=(jax.ShapeDtypeStruct((UB * BLOCK,...  9.08 us

profile of v8, /device:TPU:0, one launch (start us, length us, event | category | flops | bytes accessed | tf_op | source)
XLA Modules:
  0.0 131.4 jit_solution(17123121086980265335)
XLA Ops:
  0.7 33.4 %gather.1 = (bf16[64,128,128]{2,1,0:T(8,128)(2,1)S(1)}, bf16[64,128,128]{2,1,0:T(8,128)(2,1)S(1)}, bf16[64,128,128]{2,1,0:T(8,128)(2,1)S(1)}, bf16[64,128,128]{2...) custom-call(f32[8,128,128]{2,1,0:T(8,128)} %bitcast.28, ...), custom_call_target="tpu_custom_call" | custom-call | tf_op jit(solution)/shard_map/gather/pallas_call | solution.py:286
  34.0 0.0 copy-start
  34.0 9.1 %build.1 = (f32[2048,128]{1,0:T(8,128)S(1)}, f32[512,128,128]{2,1,0:T(8,128)}, s32[1024]{0:T(1024)S(1)}, s32[1]{0:T(128)}) custom-call(s32[16,104,512]{2,1,0:T(8,128)S(1)} %bitcast.21, bf16[64,128,128]{2,1,0:T(8,128)(2,1)S(1)} %get-tuple-element.84.yh, bf16[64,128,128]{2,1,0:T(8,128)(2,1)S(1)} %get-tuple-element.85.yl, ...), custom_call_target="tpu_custom_call" | custom-call | tf_op jit(solution)/shard_map/build/pallas_call | solution.py:436
  43.8 0.0 copy-done
  43.8 86.7 %conditional.1 = (f32[2048,128]{1,0:T(8,128)S(1)}) conditional(s32[]{:T(128)} %bitcast.17, (f32[2048,128]{1,0:T(8,128)S(1)}, s32[1024]{0:T(1024)S(1)}, f32[2048,128]{1,0:T(8,128)S(1)}, bf16[64,128,128]{2,1,0:T(8,128)(2,1)S(1)}, bf16[64,128,128]{2,1,0:T(8,128)(2,1)S(1)}, /*index=5*/bf16[64,128,128]{2,1,0:T(8,128)(2,1)S(1)}, ...), branch_computations={%region_0.0_spmd, %region_1.0_spmd} | conditional | bytes 8 | solution.py:972
  44.0 86.2 %steps.1 = f32[16,128,128]{2,1,0:T(8,128)S(1)} custom-call(s32[1024]{0:T(1024)S(1)} %get-tuple-element.63.order, f32[4,4,128,128]{3,2,1,0:T(8,128)S(1)} %bitcast.26, f32[16,128,128]{2,1,0:T(8,128)S(1)} %bitcast.24, bf16[64,128,128]{2,1,0:T(8,128)(2,1)S(1)} %get-tuple-element.66.yh, bf16[64,128,128]{2,1,0:T(8,128)(2,1)S(1)} %get-tuple-element.67.yl, ...), custom_call_target="tpu_custom_call" | custom-call | tf_op jit(solution)/shard_map/cond/branch_1_fun/steps/pallas_call | solution.py:894
  130.4 1.0 copy.16
Async XLA Ops:
  34.0 9.7 %copy-start = (f32[2048,128]{1,0:T(8,128)S(1)}, f32[2048,128]{1,0:T(8,128)}, u32[]{:S(2)}) copy-start(f32[2048,128]{1,0:T(8,128)} %start.1) | copy-start | bytes 3145732

commit v9 on v8

--- a/solution.py
+++ b/solution.py
@@ -21,7 +21,7 @@
 LIST = 1024
 LAST = 512
 FAST = 36
-STEP = 18
+STEP = 36
 SUB = 32
 THIN = 16
 UNROLL = 4

time: 132 us -> 128 us (0.970)
  Pallas kernels: 129 us -> 124 us
    pallas_call x1, Pallas kernels: 86.2 us -> 82.3 us  [all_steps(): pl.pallas_call(cg_kernel, out_shape=jax.ShapeDtypeStruct(blocks, F32), in...]
where the time goes in v9:
time: 128 us; the launch traced here: 127 us
  Pallas kernels  124 us (97%)
  between operations  1.34 us (1%)
    pallas_call x1, Pallas kernels, all_steps(): pl.pallas_call(cg_kernel, out_shape=jax.ShapeDtypeStruct(blocks, F32), in...  82.3 us
    pallas_call x1, Pallas kernels, gather(): pl.pallas_call(gather_kernel, out_shape=(*[jax.ShapeDtypeStruct((ROWS * I...  33.4 us
    pallas_call x1, Pallas kernels, build(): pl.pallas_call(build_kernel, out_shape=(jax.ShapeDtypeStruct((UB * BLOCK,...  8.32 us

profile of v9, /device:TPU:0, one launch (start us, length us, event | category | flops | bytes accessed | tf_op | source)
XLA Modules:
  0.0 126.8 jit_solution(16268128743061199650)
XLA Ops:
  0.7 33.4 %gather.1 = (bf16[64,128,128]{2,1,0:T(8,128)(2,1)S(1)}, bf16[64,128,128]{2,1,0:T(8,128)(2,1)S(1)}, bf16[64,128,128]{2,1,0:T(8,128)(2,1)S(1)}, bf16[64,128,128]{2...) custom-call(f32[8,128,128]{2,1,0:T(8,128)} %bitcast.28, ...), custom_call_target="tpu_custom_call" | custom-call | tf_op jit(solution)/shard_map/gather/pallas_call | solution.py:286
  34.0 0.0 copy-start
  34.0 8.3 %build.1 = (f32[2048,128]{1,0:T(8,128)S(1)}, f32[512,128,128]{2,1,0:T(8,128)}, s32[1024]{0:T(1024)S(1)}, s32[1]{0:T(128)}) custom-call(s32[16,104,512]{2,1,0:T(8,128)S(1)} %bitcast.21, bf16[64,128,128]{2,1,0:T(8,128)(2,1)S(1)} %get-tuple-element.84.yh, bf16[64,128,128]{2,1,0:T(8,128)(2,1)S(1)} %get-tuple-element.85.yl, ...), custom_call_target="tpu_custom_call" | custom-call | tf_op jit(solution)/shard_map/build/pallas_call | solution.py:436
  43.0 0.0 copy-done
  43.0 82.8 %conditional.1 = (f32[2048,128]{1,0:T(8,128)S(1)}) conditional(s32[]{:T(128)} %bitcast.17, (f32[2048,128]{1,0:T(8,128)S(1)}, s32[1024]{0:T(1024)S(1)}, f32[2048,128]{1,0:T(8,128)S(1)}, bf16[64,128,128]{2,1,0:T(8,128)(2,1)S(1)}, bf16[64,128,128]{2,1,0:T(8,128)(2,1)S(1)}, /*index=5*/bf16[64,128,128]{2,1,0:T(8,128)(2,1)S(1)}, ...), branch_computations={%region_0.0_spmd, %region_1.0_spmd} | conditional | bytes 8 | solution.py:972
  43.2 82.3 %steps.1 = f32[16,128,128]{2,1,0:T(8,128)S(1)} custom-call(s32[1024]{0:T(1024)S(1)} %get-tuple-element.63.order, f32[4,4,128,128]{3,2,1,0:T(8,128)S(1)} %bitcast.26, f32[16,128,128]{2,1,0:T(8,128)S(1)} %bitcast.24, bf16[64,128,128]{2,1,0:T(8,128)(2,1)S(1)} %get-tuple-element.66.yh, bf16[64,128,128]{2,1,0:T(8,128)(2,1)S(1)} %get-tuple-element.67.yl, ...), custom_call_target="tpu_custom_call" | custom-call | tf_op jit(solution)/shard_map/cond/branch_1_fun/steps/pallas_call | solution.py:894
  125.8 1.0 copy.16
Async XLA Ops:
  34.0 9.0 %copy-start = (f32[2048,128]{1,0:T(8,128)S(1)}, f32[2048,128]{1,0:T(8,128)}, u32[]{:S(2)}) copy-start(f32[2048,128]{1,0:T(8,128)} %start.1) | copy-start | bytes 3145732

commit v10 on v9

--- a/solution.py
+++ b/solution.py
@@ -210,20 +210,19 @@
             tl[at] = low.T
             return sums + dot(high_t, jnp.concatenate([high, low], axis=1), NN)
 
-        return lax.fori_loop(0, IB, one, sums, unroll=4)
+        return lax.fori_loop(0, IB, one, sums, unroll=8)
 
     loads[3].wait()
     sums = add(r, jnp.zeros((K, 2 * K), F32))
-    for copy in told_keys:
-        copy.wait_recv()
-    mine = keys.at[z]
-    told_keys = [send(mine, mine, peer) for peer in along_z]
-
     for d in (1, 3, 2):
         for w in (0, 1):
             near[w][d].wait_recv()
             rows, _, _, at = ways[w]
             spread(w, d, at(-d, 0).at[rows])
+    for copy in told_keys:
+        copy.wait_recv()
+    mine = keys.at[z]
+    told_keys = [send(mine, mine, peer) for peer in along_z]
     for w in (0, 1):
         pass_on(w, 0)
     from_left[0].wait_recv()
@@ -232,21 +231,6 @@
     from_right[1].wait_recv()
     piece = land.at[right, pl.ds(4, 4)]
     round_y.append(send(piece, piece, to_left))
-    for copy in told_keys:
-        copy.wait_recv()
-    owners = keys[:, :, 0, :].reshape(COLS, 128)
-    counted = [
-        jnp.sum(jnp.where(owners == column, 1.0, 0.0), axis=0, keepdims=True)
-        for column in range(COLS)
-    ]
-    counted = jnp.sum(jnp.concatenate(counted, axis=0), axis=1, keepdims=True)
-    longest = jnp.max(counted, axis=0, keepdims=True).astype(jnp.int32)
-    most[0] = jnp.broadcast_to(longest, (8, 128))
-
-    told = [
-        send(most.at[0], seen.at[i], peer)
-        for i, peer in enumerate((to_right, to_left, to_across))
-    ]
     between[0].wait_recv()
     sums = add(other, sums)
     for d in (1, 3):
@@ -258,12 +242,27 @@
     between.append(send(land.at[right], land.at[right], to_other))
     for w in (0, 1):
         pass_on(w, 2)
+    for copy in told_keys:
+        copy.wait_recv()
+    owners = keys[:, :, 0, :].reshape(COLS, 128)
+    counted = [
+        jnp.sum(jnp.where(owners == column, 1.0, 0.0), axis=0, keepdims=True)
+        for column in range(COLS)
+    ]
+    counted = jnp.sum(jnp.concatenate(counted, axis=0), axis=1, keepdims=True)
+    longest = jnp.max(counted, axis=0, keepdims=True).astype(jnp.int32)
+    most[0] = jnp.broadcast_to(longest, (8, 128))
+
+    told = [
+        send(most.at[0], seen.at[i], peer)
+        for i, peer in enumerate((to_right, to_left, to_across))
+    ]
+    sums = add(left, sums)
+    sums = add(right, sums)
     for copy in told:
         copy.wait_recv()
     most[1] = jnp.maximum(jnp.maximum(most[0], seen[0]), jnp.maximum(seen[1], seen[2]))
     told = send(most.at[1], seen.at[3], to_other)
-    sums = add(left, sums)
-    sums = add(right, sums)
     for copy in round_y:
         copy.wait_recv()
     between.append(send(land.at[across], land.at[across], to_other))

time: 128 us -> 130 us (1.016); the launches traced: 127 us -> 127 us
  no operation moved by 1% of the time
where the time goes in v10:
time: 130 us; the launch traced here: 127 us
  Pallas kernels  124 us (95%)
  between operations  1.34 us (1%)
    pallas_call x1, Pallas kernels, all_steps(): pl.pallas_call(cg_kernel, out_shape=jax.ShapeDtypeStruct(blocks, F32), in...  83.5 us
    pallas_call x1, Pallas kernels, gather(): pl.pallas_call(gather_kernel, out_shape=(*[jax.ShapeDtypeStruct((ROWS * I...  32.6 us
    pallas_call x1, Pallas kernels, build(): pl.pallas_call(build_kernel, out_shape=(jax.ShapeDtypeStruct((UB * BLOCK,...  8.32 us

profile of v10, /device:TPU:0, one launch (start us, length us, event | category | flops | bytes accessed | tf_op | source)
XLA Modules:
  0.0 127.2 jit_solution(5181569848834740588)
XLA Ops:
  0.7 32.6 %gather.1 = (bf16[64,128,128]{2,1,0:T(8,128)(2,1)S(1)}, bf16[64,128,128]{2,1,0:T(8,128)(2,1)S(1)}, bf16[64,128,128]{2,1,0:T(8,128)(2,1)S(1)}, bf16[64,128,128]{2...) custom-call(f32[8,128,128]{2,1,0:T(8,128)} %bitcast.28, ...), custom_call_target="tpu_custom_call" | custom-call | tf_op jit(solution)/shard_map/gather/pallas_call | solution.py:285
  33.3 0.0 copy-start
  33.3 8.3 %build.1 = (f32[2048,128]{1,0:T(8,128)S(1)}, f32[512,128,128]{2,1,0:T(8,128)}, s32[1024]{0:T(1024)S(1)}, s32[1]{0:T(128)}) custom-call(s32[16,104,512]{2,1,0:T(8,128)S(1)} %bitcast.21, bf16[64,128,128]{2,1,0:T(8,128)(2,1)S(1)} %get-tuple-element.84.yh, bf16[64,128,128]{2,1,0:T(8,128)(2,1)S(1)} %get-tuple-element.85.yl, ...), custom_call_target="tpu_custom_call" | custom-call | tf_op jit(solution)/shard_map/build/pallas_call | solution.py:435
  42.3 0.0 copy-done
  42.3 83.9 %conditional.1 = (f32[2048,128]{1,0:T(8,128)S(1)}) conditional(s32[]{:T(128)} %bitcast.17, (f32[2048,128]{1,0:T(8,128)S(1)}, s32[1024]{0:T(1024)S(1)}, f32[2048,128]{1,0:T(8,128)S(1)}, bf16[64,128,128]{2,1,0:T(8,128)(2,1)S(1)}, bf16[64,128,128]{2,1,0:T(8,128)(2,1)S(1)}, /*index=5*/bf16[64,128,128]{2,1,0:T(8,128)(2,1)S(1)}, ...), branch_computations={%region_0.0_spmd, %region_1.0_spmd} | conditional | bytes 8 | solution.py:971
  42.5 83.5 %steps.1 = f32[16,128,128]{2,1,0:T(8,128)S(1)} custom-call(s32[1024]{0:T(1024)S(1)} %get-tuple-element.63.order, f32[4,4,128,128]{3,2,1,0:T(8,128)S(1)} %bitcast.26, f32[16,128,128]{2,1,0:T(8,128)S(1)} %bitcast.24, bf16[64,128,128]{2,1,0:T(8,128)(2,1)S(1)} %get-tuple-element.66.yh, bf16[64,128,128]{2,1,0:T(8,128)(2,1)S(1)} %get-tuple-element.67.yl, ...), custom_call_target="tpu_custom_call" | custom-call | tf_op jit(solution)/shard_map/cond/branch_1_fun/steps/pallas_call | solution.py:893
  126.2 1.0 copy.16
Async XLA Ops:
  33.3 9.0 %copy-start = (f32[2048,128]{1,0:T(8,128)S(1)}, f32[2048,128]{1,0:T(8,128)}, u32[]{:S(2)}) copy-start(f32[2048,128]{1,0:T(8,128)} %start.1) | copy-start | bytes 3145732
